TPU v7x, 512 devices: a whole 4x4x16 slice. The times are simulated.
512 devices in a mesh: dp: 16 (over y, x_lo, core), ctx: 32 (over z, x_hi).
Axes of the slice: x: 4 (x_hi: 2, x_lo: 2; x = x_hi * 2 + x_lo), y: 4, z: 16, core: 2. Of those that a mesh axis runs over, the one named last changes fastest.
Arguments:
- queries: bfloat16 [16, 4096, 2048], P('dp', 'ctx'), may hold values from -8 to 8
- keys: bfloat16 [16, 4096, 2048], P('dp', 'ctx'), may hold values from -8 to 8
- values: bfloat16 [16, 4096, 2048], P('dp', 'ctx'), may hold values from -4.1875 to 4.1875
- out_grad: bfloat16 [16, 4096, 2048], P('dp', 'ctx'), may hold values from -15 to 15
- log_norm: bfloat16 [16, 4096, 16], P('dp', 'ctx'), may hold values from 6.78125 to 8.1875
- row_delta: bfloat16 [16, 4096, 16], P('dp', 'ctx'), may hold values from -48 to 48
- doc_lengths: int32 [16, 8, 4], replicated, may hold values from 0 to 4, as said below
- bin_dest: int32 [16, 8], replicated, may hold values from 0 to 15, as said below
Outputs:
- query_grad: bfloat16 [16, 4096, 2048], P('dp', 'ctx')
- key_grad: bfloat16 [16, 4096, 2048], P('dp', 'ctx')
- value_grad: bfloat16 [16, 4096, 2048], P('dp', 'ctx')
Inputs may be any that keep to these rules, and one draw needn't show every extreme that they name: doc_lengths[g, b] lists the lengths in blocks of the documents that fill bin b of row g, in order, followed by zeros; they sum to 4; some bin is a single document. bin_dest[g, b] is g or g XOR (8); where it is the other group, that group's bin b has destination g.
All inputs are finite; a program needn't handle non-finite values.
Results may differ from a plain program's by a relative error of at most 0.0085.
Values may be sent and summed in bfloat16 or wider, within the bound.
No kernel may reach another device: no remote copies, remote signals or barrier semaphores. Data moves between devices by JAX's collectives and lax.ppermute only.
A program may use at most 64 MiB of HBM per device.

v0:
```python
import math

import jax
import jax.numpy as jnp
from jax import lax
from jax.sharding import PartitionSpec as P

BLOCK = 128


def from_behind(shard, axis, by):
    devices = lax.axis_size(axis)
    pairs = [(i, i + by) for i in range(devices) if 0 <= i + by < devices]
    return lax.ppermute(shard, axis, pairs)


def partner_2(block, axis, apart):
    count = lax.axis_size(axis)
    route = []
    for low in range(count):
        high = low | 1 << apart
        if high != low and high < count:
            route += [(low, high), (high, low)]
    return lax.ppermute(block, axis, route)


def token_docs(doc_ends, first_token, token_count):
    position = first_token + jnp.arange(token_count, dtype=jnp.int32)
    block_index = position // BLOCK
    return jnp.sum((doc_ends[None, :] <= block_index[:, None]).astype(jnp.int32), axis=1)


def block_docs(doc_ends, bin_place, token_count):
    inside = (bin_place >= 0) & (bin_place < 4)
    doc_index = token_docs(doc_ends, jnp.clip(bin_place, 0, 3) * token_count, token_count)
    return jnp.where(inside, doc_index, -1)


def attend_back(
    queries, key_rows, value_rows, out_grad, log_norm, row_delta, query_doc, key_doc, head_count
):
    tok_rows, feature_count = queries.shape
    head_width = feature_count // head_count
    inv_root = 1.0 / math.sqrt(head_width)
    key_count = key_rows.shape[0]
    query_heads = queries.reshape(tok_rows, head_count, head_width)
    key_heads = key_rows.reshape(key_count, head_count, head_width)
    value_heads = value_rows.reshape(key_count, head_count, head_width)
    grad_heads = out_grad.reshape(tok_rows, head_count, head_width)
    scores = (
        jnp.einsum("qhd,khd->hqk", query_heads, key_heads, preferred_element_type=jnp.float32)
        * inv_root
    )
    norm_column = jnp.transpose(log_norm.astype(jnp.float32))[:, :, None]
    delta_column = jnp.transpose(row_delta.astype(jnp.float32))[:, :, None]
    same_doc = (query_doc[:, None] == key_doc[None, :])[None]
    probs = jnp.where(same_doc, jnp.exp(scores - norm_column), 0.0)
    probs_low = probs.astype(jnp.bfloat16)
    dprobs = jnp.einsum("qhd,khd->hqk", grad_heads, value_heads, preferred_element_type=jnp.float32)
    dscores = probs * (dprobs - delta_column)
    dscores_low = dscores.astype(jnp.bfloat16)
    query_grad = (
        (
            jnp.einsum("hqk,khd->qhd", dscores_low, key_heads, preferred_element_type=jnp.float32)
            * inv_root
        )
        .astype(jnp.bfloat16)
        .reshape(tok_rows, feature_count)
    )
    key_terms = (
        (
            jnp.einsum("hqk,qhd->khd", dscores_low, query_heads, preferred_element_type=jnp.float32)
            * inv_root
        )
        .astype(jnp.bfloat16)
        .reshape(key_count, feature_count)
    )
    value_terms = (
        jnp.einsum("hqk,qhd->khd", probs_low, grad_heads, preferred_element_type=jnp.float32)
        .astype(jnp.bfloat16)
        .reshape(key_count, feature_count)
    )
    return (query_grad, key_terms, value_terms)


def bin_gradients(
    queries, keys, values, out_grad, log_norm, row_delta, lengths_row, offset, head_count
):
    tok_rows = queries.shape[1]
    feature_count = queries.shape[2]
    doc_ends = jnp.cumsum(lengths_row)
    query_doc = token_docs(doc_ends, offset * tok_rows, tok_rows)
    own_pair = (keys[0], values[0])
    ahead_list = []
    moving = own_pair
    for repeat in range(3):
        moving = from_behind((moving[0], moving[1]), "ctx", -1)
        ahead_list.append(moving)
    behind = []
    moving = own_pair
    for repeat in range(3):
        moving = from_behind((moving[0], moving[1]), "ctx", 1)
        behind.append(moving)
    visits = behind[::-1] + [own_pair] + ahead_list
    key_stack = jnp.stack([kv_pair[0] for kv_pair in visits])
    value_stack = jnp.stack([kv_pair[1] for kv_pair in visits])
    key_doc = jnp.concatenate(
        [block_docs(doc_ends, offset + distance, tok_rows) for distance in range(-3, 4)]
    )
    query_grad, key_part, value_part = attend_back(
        queries[0],
        key_stack.reshape(7 * tok_rows, feature_count),
        value_stack.reshape(7 * tok_rows, feature_count),
        out_grad[0],
        log_norm[0],
        row_delta[0],
        query_doc,
        key_doc,
        head_count,
    )
    key_terms = key_part.reshape(7, tok_rows, feature_count)
    value_terms = value_part.reshape(7, tok_rows, feature_count)
    key_sum = lax.optimization_barrier(key_terms[3]).astype(jnp.float32)
    value_sum = lax.optimization_barrier(value_terms[3]).astype(jnp.float32)
    for distance in (-3, -2, -1, 1, 2, 3):
        returned = from_behind(
            (key_terms[3 + distance], value_terms[3 + distance]), "ctx", distance
        )
        key_sum = key_sum + returned[0].astype(jnp.float32)
        value_sum = value_sum + returned[1].astype(jnp.float32)
    return (
        query_grad[None],
        key_sum.astype(jnp.bfloat16)[None],
        value_sum.astype(jnp.bfloat16)[None],
    )


def body(queries, keys, values, out_grad, log_norm, row_delta, doc_lengths, bin_dest):
    head_count = log_norm.shape[2]
    group_index = lax.axis_index("dp")
    position = lax.axis_index("ctx")
    bin_index = position // 4
    offset = position % 4
    top_bit = lax.axis_size("dp").bit_length() - 2
    partner = jnp.bitwise_xor(group_index, 1 << top_bit)
    own_dest = bin_dest[group_index, bin_index]
    was_moved = own_dest != group_index
    staying = (queries, keys, values, out_grad, log_norm, row_delta)
    arrived = partner_2((queries, keys, values, out_grad, log_norm, row_delta), "dp", top_bit)
    chosen = [
        jnp.where(was_moved, incoming, current) for incoming, current in zip(arrived, staying)
    ]
    source = jnp.where(was_moved, partner, group_index)
    return bin_gradients(
        chosen[0],
        chosen[1],
        chosen[2],
        chosen[3],
        chosen[4],
        chosen[5],
        doc_lengths[source, bin_index],
        offset,
        head_count,
    )


def solution(mesh):
    in_specs = (
        P("dp", "ctx", None),
        P("dp", "ctx", None),
        P("dp", "ctx", None),
        P("dp", "ctx", None),
        P("dp", "ctx", None),
        P("dp", "ctx", None),
        P(),
        P(),
    )
    out_specs = (P("dp", "ctx", None), P("dp", "ctx", None), P("dp", "ctx", None))
    return jax.shard_map(body, mesh=mesh, in_specs=in_specs, out_specs=out_specs, check_vma=False)
```

profile of v0, /device:TPU:440, one launch (start us, length us, event | category | flops | bytes accessed | tf_op | source)
XLA Modules:
  0.0 365.4 jit_solution(15498278328329292737)
XLA Ops:
  3.9 4.2 %collective-permute-start.17 = (bf16[1,128,16]{1,2,0:T(8,128)(2,1)}, bf16[1,128,16]{1,2,0:T(8,128)(2,1)S(1)}, u32[]{:S(2)}, u32[]{:S(2)}) collective-permute-start(bf16[1,128,16]{1,2,0:T(8,128)(2,1)} %param.13), channel_id=1, source_target_pairs={{0,256},{256,0},{32,288},{288,32},{64,320},{320,64},{96,352},{352,... | collective-permute-start | bytes 12296 | tf_op jit(solution)/shard_map/ppermute | solution.py:24
  21.4 25.9 %collective-permute-done.10 = bf16[1,128,2048]{2,1,0:T(8,128)(2,1)S(1)} collective-permute-done((bf16[1,128,2048]{2,1,0:T(8,128)(2,1)}, bf16[1,128,2048]{2,1,0:T(8,128)(2,1)S(1)}, u32[]{:S(2)}, u32[]{:S(2)}) %collective-permute-start.10) | collective-permute-done | bytes 524320 | tf_op jit(solution)/shard_map/ppermute | solution.py:24
  47.4 4.9 %collective-permute-start.11 = (bf16[128,2048]{1,0:T(8,128)(2,1)S(1)}, bf16[128,2048]{1,0:T(8,128)(2,1)S(1)}, u32[]{:S(2)}, u32[]{:S(2)}) collective-permute-start(bf16[128,2048]{1,0:T(8,128)(2,1)S(1)} %fusion.20), channel_id=1, source_target_pairs={{0,1},{1,2},{2,3},{3,4},{4,5},{5,6},{6,7},{7,8},{8,9},{9,10},{10,1... | collective-permute-start | bytes 1572872 | tf_op jit(solution)/shard_map/ppermute | solution.py:14
  63.0 4.2 %collective-permute-start.14 = (bf16[128,2048]{1,0:T(8,128)(2,1)S(1)}, bf16[128,2048]{1,0:T(8,128)(2,1)}, u32[]{:S(2)}, u32[]{:S(2)}) collective-permute-start(bf16[128,2048]{1,0:T(8,128)(2,1)S(1)} %fusion.20), channel_id=1, source_target_pairs={{1,0},{2,1},{3,2},{4,3},{5,4},{6,5},{7,6},{8,7},{9,8},{10,9},{11,1... | collective-permute-start | bytes 1572872 | tf_op jit(solution)/shard_map/ppermute | solution.py:14
  67.2 19.9 %collective-permute-done.11 = bf16[128,2048]{1,0:T(8,128)(2,1)S(1)} collective-permute-done((bf16[128,2048]{1,0:T(8,128)(2,1)S(1)}, bf16[128,2048]{1,0:T(8,128)(2,1)S(1)}, u32[]{:S(2)}, u32[]{:S(2)}) %collective-permute-start.11) | collective-permute-done | bytes 524320 | tf_op jit(solution)/shard_map/ppermute | solution.py:14
  87.2 5.9 %collective-permute-start.12 = (bf16[128,2048]{1,0:T(8,128)(2,1)S(1)}, bf16[128,2048]{1,0:T(8,128)(2,1)}, u32[]{:S(2)}, u32[]{:S(2)}) collective-permute-start(bf16[128,2048]{1,0:T(8,128)(2,1)S(1)} %collective-permute-done.11), channel_id=1, source_target_pairs={{0,1},{1,2},{2,3},{3,4},{4,5},{5,6},{6,7},{7,8},{8,9},{9,10},{10,1... | collective-permute-start | bytes 1572872 | tf_op jit(solution)/shard_map/ppermute | solution.py:14
  95.8 13.9 %collective-permute-done.1 = bf16[128,2048]{1,0:T(8,128)(2,1)} collective-permute-done((bf16[128,2048]{1,0:T(8,128)(2,1)S(1)}, bf16[128,2048]{1,0:T(8,128)(2,1)}, u32[]{:S(2)}, u32[]{:S(2)}) %collective-permute-start.1) | collective-permute-done | bytes 524320 | tf_op jit(solution)/shard_map/ppermute | solution.py:14
  109.6 6.0 %collective-permute-start.2 = (bf16[128,2048]{1,0:T(8,128)(2,1)}, bf16[128,2048]{1,0:T(8,128)(2,1)}, u32[]{:S(2)}, u32[]{:S(2)}) collective-permute-start(bf16[128,2048]{1,0:T(8,128)(2,1)} %collective-permute-done.1), channel_id=1, source_target_pairs={{0,1},{1,2},{2,3},{3,4},{4,5},{5,6},{6,7},{7,8},{8,9},{9,10},{10,1... | collective-permute-start | bytes 1572872 | tf_op jit(solution)/shard_map/ppermute | solution.py:14
  118.0 14.1 %collective-permute-done.12 = bf16[128,2048]{1,0:T(8,128)(2,1)} collective-permute-done((bf16[128,2048]{1,0:T(8,128)(2,1)S(1)}, bf16[128,2048]{1,0:T(8,128)(2,1)}, u32[]{:S(2)}, u32[]{:S(2)}) %collective-permute-start.12) | collective-permute-done | bytes 524320 | tf_op jit(solution)/shard_map/ppermute | solution.py:14
  132.1 6.0 %collective-permute-start.13 = (bf16[128,2048]{1,0:T(8,128)(2,1)}, bf16[128,2048]{1,0:T(8,128)(2,1)}, u32[]{:S(2)}, u32[]{:S(2)}) collective-permute-start(bf16[128,2048]{1,0:T(8,128)(2,1)} %collective-permute-done.12), channel_id=1, source_target_pairs={{0,1},{1,2},{2,3},{3,4},{4,5},{5,6},{6,7},{7,8},{8,9},{9,10},{10,1... | collective-permute-start | bytes 1572872 | tf_op jit(solution)/shard_map/ppermute | solution.py:14
  142.3 12.4 %collective-permute-done.2 = bf16[128,2048]{1,0:T(8,128)(2,1)} collective-permute-done((bf16[128,2048]{1,0:T(8,128)(2,1)}, bf16[128,2048]{1,0:T(8,128)(2,1)}, u32[]{:S(2)}, u32[]{:S(2)}) %collective-permute-start.2) | collective-permute-done | bytes 524320 | tf_op jit(solution)/shard_map/ppermute | solution.py:14
  154.7 5.9 %collective-permute-start.3 = (bf16[128,2048]{1,0:T(8,128)(2,1)}, bf16[128,2048]{1,0:T(8,128)(2,1)S(1)}, u32[]{:S(2)}, u32[]{:S(2)}) collective-permute-start(bf16[128,2048]{1,0:T(8,128)(2,1)} %collective-permute-done.2), channel_id=1, source_target_pairs={{0,1},{1,2},{2,3},{3,4},{4,5},{5,6},{6,7},{7,8},{8,9},{9,10},{10,1... | collective-permute-start | bytes 1572872 | tf_op jit(solution)/shard_map/ppermute | solution.py:14
  163.2 13.9 %collective-permute-done.13 = bf16[128,2048]{1,0:T(8,128)(2,1)} collective-permute-done((bf16[128,2048]{1,0:T(8,128)(2,1)}, bf16[128,2048]{1,0:T(8,128)(2,1)}, u32[]{:S(2)}, u32[]{:S(2)}) %collective-permute-start.13) | collective-permute-done | bytes 524320 | tf_op jit(solution)/shard_map/ppermute | solution.py:14
  197.7 6.4 %copy.57 = bf16[896,16,128]{0,2,1:T(8,128)(2,1)} copy(bf16[896,16,128]{2,1,0:T(8,128)(2,1)} %bitcast.82) | data formatting | bytes 7340032 | tf_op jit(solution)/shard_map/reshape;reshape | solution.py:47
  221.4 8.9 %collective-permute-start.18 = (bf16[128,2048]{1,0:T(8,128)(2,1)}, bf16[128,2048]{1,0:T(8,128)(2,1)}, u32[]{:S(2)}, u32[]{:S(2)}) collective-permute-start(bf16[128,2048]{1,0:T(8,128)(2,1)} %copy.60), channel_id=1, source_target_pairs={{3,0},{4,1},{5,2},{6,3},{7,4},{8,5},{9,6},{10,7},{11,8},{12,9},{13... | collective-permute-start | bytes 1572872 | tf_op jit(solution)/shard_map/ppermute | solution.py:14
  245.5 6.2 %collective-permute-start.26 = (bf16[128,2048]{1,0:T(8,128)(2,1)}, bf16[128,2048]{1,0:T(8,128)(2,1)}, u32[]{:S(2)}, u32[]{:S(2)}) collective-permute-start(bf16[128,2048]{1,0:T(8,128)(2,1)} %copy.70), channel_id=1, source_target_pairs={{1,0},{2,1},{3,2},{4,3},{5,4},{6,5},{7,6},{8,7},{9,8},{10,9},{11,1... | collective-permute-start | bytes 1572872 | tf_op jit(solution)/shard_map/ppermute | solution.py:14
  255.8 7.5 %collective-permute-start.28 = (bf16[128,2048]{1,0:T(8,128)(2,1)}, bf16[128,2048]{1,0:T(8,128)(2,1)}, u32[]{:S(2)}, u32[]{:S(2)}) collective-permute-start(bf16[128,2048]{1,0:T(8,128)(2,1)} %copy.72), channel_id=1, source_target_pairs={{0,2},{1,3},{2,4},{3,5},{4,6},{5,7},{6,8},{7,9},{8,10},{9,11},{10,... | collective-permute-start | bytes 1572872 | tf_op jit(solution)/shard_map/ppermute | solution.py:14
  263.3 12.9 %collective-permute-done.24 = bf16[128,2048]{1,0:T(8,128)(2,1)} collective-permute-done((bf16[128,2048]{1,0:T(8,128)(2,1)}, bf16[128,2048]{1,0:T(8,128)(2,1)}, u32[]{:S(2)}, u32[]{:S(2)}) %collective-permute-start.24) | collective-permute-done | bytes 524320 | tf_op jit(solution)/shard_map/ppermute | solution.py:14
  278.3 5.3 %fusion.14 = bf16[16,128,128]{2,1,0:T(8,128)(2,1)} fusion(bf16[896,16,128]{0,2,1:T(8,128)(2,1)} %copy.57, bf16[16,128,896]{2,1,0:T(8,128)(2,1)} %copy-done.2), kind=kOutput, calls=%fused_computation.14 | convolution fusion | flops 470286336 | bytes 7864320 | tf_op jit(solution)/shard_map/hqk,khd->qhd/dot_general | solution.py:64
  292.6 11.8 %collective-permute-done.26 = bf16[128,2048]{1,0:T(8,128)(2,1)} collective-permute-done((bf16[128,2048]{1,0:T(8,128)(2,1)}, bf16[128,2048]{1,0:T(8,128)(2,1)}, u32[]{:S(2)}, u32[]{:S(2)}) %collective-permute-start.26) | collective-permute-done | bytes 524320 | tf_op jit(solution)/shard_map/ppermute | solution.py:14
  304.3 6.8 %collective-permute-start.20 = (bf16[128,2048]{1,0:T(8,128)(2,1)S(1)}, bf16[128,2048]{1,0:T(8,128)(2,1)S(1)}, u32[]{:S(2)}, u32[]{:S(2)}) collective-permute-start(bf16[128,2048]{1,0:T(8,128)(2,1)S(1)} %copy.62), channel_id=1, source_target_pairs={{1,0},{2,1},{3,2},{4,3},{5,4},{6,5},{7,6},{8,7},{9,8},{10,9},{11,1... | collective-permute-start | bytes 1572872 | tf_op jit(solution)/shard_map/ppermute | solution.py:14
  320.2 5.6 %collective-permute-done.20 = bf16[128,2048]{1,0:T(8,128)(2,1)S(1)} collective-permute-done((bf16[128,2048]{1,0:T(8,128)(2,1)S(1)}, bf16[128,2048]{1,0:T(8,128)(2,1)S(1)}, u32[]{:S(2)}, u32[]{:S(2)}) %collective-permute-start.20) | collective-permute-done | bytes 524320 | tf_op jit(solution)/shard_map/ppermute | solution.py:14
  325.8 15.9 %collective-permute-done.21 = bf16[128,2048]{1,0:T(8,128)(2,1)S(1)} collective-permute-done((bf16[128,2048]{1,0:T(8,128)(2,1)}, bf16[128,2048]{1,0:T(8,128)(2,1)S(1)}, u32[]{:S(2)}, u32[]{:S(2)}) %collective-permute-start.21) | collective-permute-done | bytes 524320 | tf_op jit(solution)/shard_map/ppermute | solution.py:14
  341.7 21.3 %collective-permute-done.23 = bf16[128,2048]{1,0:T(8,128)(2,1)S(1)} collective-permute-done((bf16[128,2048]{1,0:T(8,128)(2,1)S(1)}, bf16[128,2048]{1,0:T(8,128)(2,1)S(1)}, u32[]{:S(2)}, u32[]{:S(2)}) %collective-permute-start.23) | collective-permute-done | bytes 524320 | tf_op jit(solution)/shard_map/ppermute | solution.py:14
  (123 shorter events, 117.4 us)
Async XLA Ops:
  0.7 54.9 %collective-permute-start.8 = (bf16[1,128,16]{1,2,0:T(8,128)(2,1)}, bf16[1,128,16]{1,2,0:T(8,128)(2,1)S(1)}, u32[]{:S(2)}, u32[]{:S(2)}) collective-permute-start(bf16[1,128,16]{1,2,0:T(8,128)(2,1)} %param.12), channel_id=1, source_target_pairs={{0,256},{256,0},{32,288},{288,32},{64,320},{320,64},{96,352},{352,... | collective-permute-start | bytes 12296 | tf_op jit(solution)/shard_map/ppermute | solution.py:24
  3.9 55.0 %collective-permute-start.17 = (bf16[1,128,16]{1,2,0:T(8,128)(2,1)}, bf16[1,128,16]{1,2,0:T(8,128)(2,1)S(1)}, u32[]{:S(2)}, u32[]{:S(2)}) collective-permute-start(bf16[1,128,16]{1,2,0:T(8,128)(2,1)} %param.13), channel_id=1, source_target_pairs={{0,256},{256,0},{32,288},{288,32},{64,320},{320,64},{96,352},{352,... | collective-permute-start | bytes 12296 | tf_op jit(solution)/shard_map/ppermute | solution.py:24
  8.2 54.8 %collective-permute-start.7 = (bf16[1,128,2048]{2,1,0:T(8,128)(2,1)}, bf16[1,128,2048]{2,1,0:T(8,128)(2,1)S(1)}, u32[]{:S(2)}, u32[]{:S(2)}) collective-permute-start(bf16[1,128,2048]{2,1,0:T(8,128)(2,1)} %param.8), channel_id=1, source_target_pairs={{0,256},{256,0},{32,288},{288,32},{64,320},{320,64},{96,352},{352,... | collective-permute-start | bytes 1572872 | tf_op jit(solution)/shard_map/ppermute | solution.py:24
  11.3 41.1 %collective-permute-start = (bf16[1,128,2048]{2,1,0:T(8,128)(2,1)}, bf16[1,128,2048]{2,1,0:T(8,128)(2,1)S(1)}, u32[]{:S(2)}, u32[]{:S(2)}) collective-permute-start(bf16[1,128,2048]{2,1,0:T(8,128)(2,1)} %param.9), channel_id=1, source_target_pairs={{0,256},{256,0},{32,288},{288,32},{64,320},{320,64},{96,352},{352,... | collective-permute-start | bytes 1572872 | tf_op jit(solution)/shard_map/ppermute | solution.py:24
  15.5 31.8 %collective-permute-start.10 = (bf16[1,128,2048]{2,1,0:T(8,128)(2,1)}, bf16[1,128,2048]{2,1,0:T(8,128)(2,1)S(1)}, u32[]{:S(2)}, u32[]{:S(2)}) collective-permute-start(bf16[1,128,2048]{2,1,0:T(8,128)(2,1)} %param.10), channel_id=1, source_target_pairs={{0,256},{256,0},{32,288},{288,32},{64,320},{320,64},{96,352},{352,... | collective-permute-start | bytes 1572872 | tf_op jit(solution)/shard_map/ppermute | solution.py:24
  47.4 39.8 %collective-permute-start.11 = (bf16[128,2048]{1,0:T(8,128)(2,1)S(1)}, bf16[128,2048]{1,0:T(8,128)(2,1)S(1)}, u32[]{:S(2)}, u32[]{:S(2)}) collective-permute-start(bf16[128,2048]{1,0:T(8,128)(2,1)S(1)} %fusion.20), channel_id=1, source_target_pairs={{0,1},{1,2},{2,3},{3,4},{4,5},{5,6},{6,7},{7,8},{8,9},{9,10},{10,1... | collective-permute-start | bytes 1572872 | tf_op jit(solution)/shard_map/ppermute | solution.py:14
  52.4 85.8 %collective-permute-start.9 = (bf16[1,128,2048]{2,1,0:T(8,128)(2,1)}, bf16[1,128,2048]{2,1,0:T(8,128)(2,1)S(1)}, u32[]{:S(2)}, u32[]{:S(2)}) collective-permute-start(bf16[1,128,2048]{2,1,0:T(8,128)(2,1)} %param.11), channel_id=1, source_target_pairs={{0,256},{256,0},{32,288},{288,32},{64,320},{320,64},{96,352},{352,... | collective-permute-start | bytes 1572872 | tf_op jit(solution)/shard_map/ppermute | solution.py:24
  55.6 37.7 %collective-permute-start.4 = (bf16[128,2048]{1,0:T(8,128)(2,1)S(1)}, bf16[128,2048]{1,0:T(8,128)(2,1)}, u32[]{:S(2)}, u32[]{:S(2)}) collective-permute-start(bf16[128,2048]{1,0:T(8,128)(2,1)S(1)} %fusion.18), channel_id=1, source_target_pairs={{1,0},{2,1},{3,2},{4,3},{5,4},{6,5},{7,6},{8,7},{9,8},{10,9},{11,1... | collective-permute-start | bytes 1572872 | tf_op jit(solution)/shard_map/ppermute | solution.py:14
  58.9 50.7 %collective-permute-start.1 = (bf16[128,2048]{1,0:T(8,128)(2,1)S(1)}, bf16[128,2048]{1,0:T(8,128)(2,1)}, u32[]{:S(2)}, u32[]{:S(2)}) collective-permute-start(bf16[128,2048]{1,0:T(8,128)(2,1)S(1)} %fusion.18), channel_id=1, source_target_pairs={{0,1},{1,2},{2,3},{3,4},{4,5},{5,6},{6,7},{7,8},{8,9},{9,10},{10,1... | collective-permute-start | bytes 1572872 | tf_op jit(solution)/shard_map/ppermute | solution.py:14
  63.0 52.6 %collective-permute-start.14 = (bf16[128,2048]{1,0:T(8,128)(2,1)S(1)}, bf16[128,2048]{1,0:T(8,128)(2,1)}, u32[]{:S(2)}, u32[]{:S(2)}) collective-permute-start(bf16[128,2048]{1,0:T(8,128)(2,1)S(1)} %fusion.20), channel_id=1, source_target_pairs={{1,0},{2,1},{3,2},{4,3},{5,4},{6,5},{7,6},{8,7},{9,8},{10,9},{11,1... | collective-permute-start | bytes 1572872 | tf_op jit(solution)/shard_map/ppermute | solution.py:14
  87.2 44.9 %collective-permute-start.12 = (bf16[128,2048]{1,0:T(8,128)(2,1)S(1)}, bf16[128,2048]{1,0:T(8,128)(2,1)}, u32[]{:S(2)}, u32[]{:S(2)}) collective-permute-start(bf16[128,2048]{1,0:T(8,128)(2,1)S(1)} %collective-permute-done.11), channel_id=1, source_target_pairs={{0,1},{1,2},{2,3},{3,4},{4,5},{5,6},{6,7},{7,8},{8,9},{9,10},{10,1... | collective-permute-start | bytes 1572872 | tf_op jit(solution)/shard_map/ppermute | solution.py:14
  93.3 46.7 %collective-permute-start.5 = (bf16[128,2048]{1,0:T(8,128)(2,1)}, bf16[128,2048]{1,0:T(8,128)(2,1)}, u32[]{:S(2)}, u32[]{:S(2)}) collective-permute-start(bf16[128,2048]{1,0:T(8,128)(2,1)} %collective-permute-done.4), channel_id=1, source_target_pairs={{1,0},{2,1},{3,2},{4,3},{5,4},{6,5},{7,6},{8,7},{9,8},{10,9},{11,1... | collective-permute-start | bytes 1572872 | tf_op jit(solution)/shard_map/ppermute | solution.py:14
  109.6 45.0 %collective-permute-start.2 = (bf16[128,2048]{1,0:T(8,128)(2,1)}, bf16[128,2048]{1,0:T(8,128)(2,1)}, u32[]{:S(2)}, u32[]{:S(2)}) collective-permute-start(bf16[128,2048]{1,0:T(8,128)(2,1)} %collective-permute-done.1), channel_id=1, source_target_pairs={{0,1},{1,2},{2,3},{3,4},{4,5},{5,6},{6,7},{7,8},{8,9},{9,10},{10,1... | collective-permute-start | bytes 1572872 | tf_op jit(solution)/shard_map/ppermute | solution.py:14
  115.7 44.9 %collective-permute-start.15 = (bf16[128,2048]{1,0:T(8,128)(2,1)}, bf16[128,2048]{1,0:T(8,128)(2,1)}, u32[]{:S(2)}, u32[]{:S(2)}) collective-permute-start(bf16[128,2048]{1,0:T(8,128)(2,1)} %collective-permute-done.14), channel_id=1, source_target_pairs={{1,0},{2,1},{3,2},{4,3},{5,4},{6,5},{7,6},{8,7},{9,8},{10,9},{11,1... | collective-permute-start | bytes 1572872 | tf_op jit(solution)/shard_map/ppermute | solution.py:14
  132.1 45.0 %collective-permute-start.13 = (bf16[128,2048]{1,0:T(8,128)(2,1)}, bf16[128,2048]{1,0:T(8,128)(2,1)}, u32[]{:S(2)}, u32[]{:S(2)}) collective-permute-start(bf16[128,2048]{1,0:T(8,128)(2,1)} %collective-permute-done.12), channel_id=1, source_target_pairs={{0,1},{1,2},{2,3},{3,4},{4,5},{5,6},{6,7},{7,8},{8,9},{9,10},{10,1... | collective-permute-start | bytes 1572872 | tf_op jit(solution)/shard_map/ppermute | solution.py:14
  139.9 54.5 %collective-permute-start.6 = (bf16[128,2048]{1,0:T(8,128)(2,1)}, bf16[128,2048]{1,0:T(8,128)(2,1)S(1)}, u32[]{:S(2)}, u32[]{:S(2)}) collective-permute-start(bf16[128,2048]{1,0:T(8,128)(2,1)} %collective-permute-done.5), channel_id=1, source_target_pairs={{1,0},{2,1},{3,2},{4,3},{5,4},{6,5},{7,6},{8,7},{9,8},{10,9},{11,1... | collective-permute-start | bytes 1572872 | tf_op jit(solution)/shard_map/ppermute | solution.py:14
  221.4 34.3 %collective-permute-start.18 = (bf16[128,2048]{1,0:T(8,128)(2,1)}, bf16[128,2048]{1,0:T(8,128)(2,1)}, u32[]{:S(2)}, u32[]{:S(2)}) collective-permute-start(bf16[128,2048]{1,0:T(8,128)(2,1)} %copy.60), channel_id=1, source_target_pairs={{3,0},{4,1},{5,2},{6,3},{7,4},{8,5},{9,6},{10,7},{11,8},{12,9},{13... | collective-permute-start | bytes 1572872 | tf_op jit(solution)/shard_map/ppermute | solution.py:14
  232.4 43.8 %collective-permute-start.24 = (bf16[128,2048]{1,0:T(8,128)(2,1)}, bf16[128,2048]{1,0:T(8,128)(2,1)}, u32[]{:S(2)}, u32[]{:S(2)}) collective-permute-start(bf16[128,2048]{1,0:T(8,128)(2,1)} %copy.68), channel_id=1, source_target_pairs={{3,0},{4,1},{5,2},{6,3},{7,4},{8,5},{9,6},{10,7},{11,8},{12,9},{13... | collective-permute-start | bytes 1572872 | tf_op jit(solution)/shard_map/ppermute | solution.py:14
  242.6 48.0 %collective-permute-start.25 = (bf16[128,2048]{1,0:T(8,128)(2,1)}, bf16[128,2048]{1,0:T(8,128)(2,1)}, u32[]{:S(2)}, u32[]{:S(2)}) collective-permute-start(bf16[128,2048]{1,0:T(8,128)(2,1)} %copy.69), channel_id=1, source_target_pairs={{2,0},{3,1},{4,2},{5,3},{6,4},{7,5},{8,6},{9,7},{10,8},{11,9},{12,... | collective-permute-start | bytes 1572872 | tf_op jit(solution)/shard_map/ppermute | solution.py:14
  245.5 58.8 %collective-permute-start.26 = (bf16[128,2048]{1,0:T(8,128)(2,1)}, bf16[128,2048]{1,0:T(8,128)(2,1)}, u32[]{:S(2)}, u32[]{:S(2)}) collective-permute-start(bf16[128,2048]{1,0:T(8,128)(2,1)} %copy.70), channel_id=1, source_target_pairs={{1,0},{2,1},{3,2},{4,3},{5,4},{6,5},{7,6},{8,7},{9,8},{10,9},{11,1... | collective-permute-start | bytes 1572872 | tf_op jit(solution)/shard_map/ppermute | solution.py:14
  253.8 57.3 %collective-permute-start.27 = (bf16[128,2048]{1,0:T(8,128)(2,1)}, bf16[128,2048]{1,0:T(8,128)(2,1)}, u32[]{:S(2)}, u32[]{:S(2)}) collective-permute-start(bf16[128,2048]{1,0:T(8,128)(2,1)} %copy.71), channel_id=1, source_target_pairs={{0,1},{1,2},{2,3},{3,4},{4,5},{5,6},{6,7},{7,8},{8,9},{9,10},{10,1... | collective-permute-start | bytes 1572872 | tf_op jit(solution)/shard_map/ppermute | solution.py:14
  255.8 57.3 %collective-permute-start.28 = (bf16[128,2048]{1,0:T(8,128)(2,1)}, bf16[128,2048]{1,0:T(8,128)(2,1)}, u32[]{:S(2)}, u32[]{:S(2)}) collective-permute-start(bf16[128,2048]{1,0:T(8,128)(2,1)} %copy.72), channel_id=1, source_target_pairs={{0,2},{1,3},{2,4},{3,5},{4,6},{5,7},{6,8},{7,9},{8,10},{9,11},{10,... | collective-permute-start | bytes 1572872 | tf_op jit(solution)/shard_map/ppermute | solution.py:14
  276.2 38.9 %collective-permute-start.29 = (bf16[128,2048]{1,0:T(8,128)(2,1)}, bf16[128,2048]{1,0:T(8,128)(2,1)}, u32[]{:S(2)}, u32[]{:S(2)}) collective-permute-start(bf16[128,2048]{1,0:T(8,128)(2,1)} %copy.73), channel_id=1, source_target_pairs={{0,3},{1,4},{2,5},{3,6},{4,7},{5,8},{6,9},{7,10},{8,11},{9,12},{10... | collective-permute-start | bytes 1572872 | tf_op jit(solution)/shard_map/ppermute | solution.py:14
  315.0 48.0 %collective-permute-start.23 = (bf16[128,2048]{1,0:T(8,128)(2,1)S(1)}, bf16[128,2048]{1,0:T(8,128)(2,1)S(1)}, u32[]{:S(2)}, u32[]{:S(2)}) collective-permute-start(bf16[128,2048]{1,0:T(8,128)(2,1)S(1)} %copy.65), channel_id=1, source_target_pairs={{0,3},{1,4},{2,5},{3,6},{4,7},{5,8},{6,9},{7,10},{8,11},{9,12},{10... | collective-permute-start | bytes 1572872 | tf_op jit(solution)/shard_map/ppermute | solution.py:14
  (17 other events, 820.0 us)
where the time goes:
time: 368 us; the launch traced here: 365 us
  waiting for transfers between devices  172 us (47%)
  starting transfers between devices  117 us (32%)
  local copies, waits for them, and re-layouts  50.6 us (14%)
  matrix products  15.9 us (4%)
  other arithmetic  7.78 us (2%)
    ppermute x24, waiting for transfers between devices, from_behind(): return lax.ppermute(shard, axis, pairs)  146 us
    ppermute x24, starting transfers between devices, from_behind(): return lax.ppermute(shard, axis, pairs)  96.1 us
    ppermute x6, waiting for transfers between devices, partner_2(): return lax.ppermute(block, axis, route)  25.9 us
    ppermute x6, starting transfers between devices, partner_2(): return lax.ppermute(block, axis, route)  21.1 us
    unnamed x35, local copies, waits for them, and re-layouts  18.8 us
    squeeze x6, local copies, waits for them, and re-layouts, bin_gradients(): value_terms[3 + distance]  12.3 us
  transfers between devices with their start and end apart: 30, of which 12 were waited for; matrix products, arithmetic and copies ran while one was open for 12% of the time, Pallas kernels for 0%

commit v1 on v0

v1 whole, which is shorter than its diff:
```python
import functools
import math

import jax
import jax.numpy as jnp
from jax import lax
from jax.experimental import pallas as pl
from jax.experimental.pallas import tpu as pltpu
from jax.sharding import Mesh
from jax.sharding import PartitionSpec as P

TOK = 128
HEAD = 128
SIDES = 2
SPOTS = 4
TEAM = SIDES * SPOTS
STAT_ROWS = 16
IN_ROWS = 4 * TOK + STAT_ROWS
OUT_ROWS = 3 * TOK
MASKED = -1e30
ROOT = 1.0 / math.sqrt(HEAD)
LOG2E = math.log2(math.e)


def pack_kernel(q_ref, k_ref, v_ref, g_ref, norm_ref, delta_ref, out_ref, stats, sems, stat_sem):
    width = out_ref.shape[2]
    copies = []
    for member in range(TEAM):
        for slot, ref in enumerate((q_ref, k_ref, v_ref, g_ref)):
            copy = pltpu.make_async_copy(
                ref.at[0, :, pl.ds(member * width, width)],
                out_ref.at[member, pl.ds(slot * TOK, TOK), :],
                sems.at[member, slot],
            )
            copy.start()
            copies.append(copy)
    heads = norm_ref.shape[0]
    norm = norm_ref[...].astype(jnp.float32)
    delta = delta_ref[...].astype(jnp.float32)
    row = lax.broadcasted_iota(jnp.int32, (STAT_ROWS, HEAD), 0)
    per_member = heads // TEAM
    for head in range(heads):
        tile = jnp.where(row == 0, norm[head : head + 1], 0.0)
        tile = jnp.where(row == 1, delta[head : head + 1], tile)
        place = head % per_member * HEAD
        stats[head // per_member, :, place : place + HEAD] = tile.astype(jnp.bfloat16)
    copy = pltpu.make_async_copy(stats, out_ref.at[:, pl.ds(4 * TOK, STAT_ROWS), :], stat_sem)
    copy.start()
    copies.append(copy)
    for copy in copies:
        copy.wait()


def pack(q, k, v, g, norm, delta):
    width = q.shape[2] // TEAM
    anywhere = pl.BlockSpec(memory_space=pl.ANY)
    local = pl.BlockSpec(memory_space=pltpu.VMEM)
    return pl.pallas_call(
        pack_kernel,
        out_shape=jax.ShapeDtypeStruct((TEAM, IN_ROWS, width), jnp.bfloat16),
        in_specs=[anywhere] * 4 + [local] * 2,
        out_specs=anywhere,
        scratch_shapes=[
            pltpu.VMEM((TEAM, STAT_ROWS, width), jnp.bfloat16),
            pltpu.SemaphoreType.DMA((TEAM, 4)),
            pltpu.SemaphoreType.DMA,
        ],
        name="pack",
    )(q, k, v, g, norm, delta)


def nt(a, b):
    return lax.dot_general(a, b, (((1,), (1,)), ((), ())), preferred_element_type=jnp.float32)


def nn(a, b):
    return jnp.dot(a, b, preferred_element_type=jnp.float32)


def attend_kernel(swap_ref, docs_ref, in_ref, out_ref, ds_ref):
    side = pl.program_id(0)
    span = SPOTS * TOK

    def whole(slot):
        return in_ref[:, slot * TOK : (slot + 1) * TOK, :].reshape(span, HEAD)

    q, k, v, g = (whole(slot) for slot in range(4))
    stats = [in_ref[spot, 4 * TOK :, :].astype(jnp.float32) for spot in range(SPOTS)]
    delta = jnp.concatenate([stat[1:2] for stat in stats], axis=1)
    for key_spot in range(SPOTS):
        rows = slice(key_spot * TOK, (key_spot + 1) * TOK)
        key_doc = docs_ref[side, key_spot]
        bias = jnp.concatenate(
            [
                jnp.where(docs_ref[side, spot] == key_doc, stats[spot][0:1] * -LOG2E, MASKED)
                for spot in range(SPOTS)
            ],
            axis=1,
        )
        probs = jnp.exp2(nt(k[rows], q) * (ROOT * LOG2E) + bias)
        dscores = (probs * (nt(v[rows], g) - delta)).astype(jnp.bfloat16)
        ds_ref[rows, :] = dscores
        out_ref[key_spot, TOK : 2 * TOK, :] = (nn(dscores, q) * ROOT).astype(jnp.bfloat16)
        out_ref[key_spot, 2 * TOK :, :] = nn(probs.astype(jnp.bfloat16), g).astype(jnp.bfloat16)
    dq = (nn(k.T, ds_ref[...]) * ROOT).T.astype(jnp.bfloat16)
    for spot in range(SPOTS):
        out_ref[spot, :TOK, :] = dq[spot * TOK : (spot + 1) * TOK]


def attend(swap, docs, messages):
    per_member = messages.shape[2] // HEAD
    return pl.pallas_call(
        attend_kernel,
        out_shape=jax.ShapeDtypeStruct((TEAM, OUT_ROWS, per_member * HEAD), jnp.bfloat16),
        grid_spec=pltpu.PrefetchScalarGridSpec(
            num_scalar_prefetch=2,
            grid=(SIDES, per_member),
            in_specs=[
                pl.BlockSpec((SPOTS, IN_ROWS, HEAD), lambda side, head, swap, docs: (side, 0, head))
            ],
            out_specs=pl.BlockSpec(
                (SPOTS, OUT_ROWS, HEAD),
                lambda side, head, swap, docs: (jnp.bitwise_xor(side, swap[0]), 0, head),
            ),
            scratch_shapes=[pltpu.VMEM((SPOTS * TOK, SPOTS * TOK), jnp.bfloat16)],
        ),
        name="attend",
    )(swap, docs, messages)


def unpack_kernel(in_ref, q_ref, k_ref, v_ref, sems):
    width = in_ref.shape[2]
    copies = []
    for member in range(TEAM):
        for slot, ref in enumerate((q_ref, k_ref, v_ref)):
            copy = pltpu.make_async_copy(
                in_ref.at[member, pl.ds(slot * TOK, TOK), :],
                ref.at[0, :, pl.ds(member * width, width)],
                sems.at[member, slot],
            )
            copy.start()
            copies.append(copy)
    for copy in copies:
        copy.wait()


def unpack(messages):
    anywhere = pl.BlockSpec(memory_space=pl.ANY)
    shape = jax.ShapeDtypeStruct((1, TOK, TEAM * messages.shape[2]), jnp.bfloat16)
    return pl.pallas_call(
        unpack_kernel,
        out_shape=(shape,) * 3,
        in_specs=[anywhere],
        out_specs=(anywhere,) * 3,
        scratch_shapes=[pltpu.SemaphoreType.DMA((TEAM, 3))],
        name="unpack",
    )(messages)


def body(q, k, v, g, norm, delta, doc_lengths, bin_dest):
    groups = lax.axis_size("low")
    low = lax.axis_index("low")
    bin_index = lax.axis_index("bin")
    swap = (bin_dest[low, bin_index] != low).astype(jnp.int32)[None]
    lengths = doc_lengths.reshape((SIDES, groups) + doc_lengths.shape[1:])[:, low, bin_index]
    ends = jnp.cumsum(lengths, axis=1)
    docs = jnp.sum(
        (ends[:, None, :] <= jnp.arange(SPOTS, dtype=jnp.int32)[None, :, None]).astype(jnp.int32),
        axis=2,
    )
    team = ("side", "spot")
    packed = pack(q, k, v, g, jnp.transpose(norm[0]), jnp.transpose(delta[0]))
    messages = lax.all_to_all(packed, team, 0, 0, tiled=True)
    grads = lax.all_to_all(attend(swap, docs, messages), team, 0, 0, tiled=True)
    return unpack(grads)


def solution(mesh):
    dp, ctx = mesh.devices.shape
    fine = Mesh(
        mesh.devices.reshape(SIDES, dp // SIDES, ctx // SPOTS, SPOTS),
        ("side", "low", "bin", "spot"),
    )
    split = P(("side", "low"), ("bin", "spot"), None)
    return jax.shard_map(
        body,
        mesh=fine,
        in_specs=(split,) * 6 + (P(), P()),
        out_specs=(split,) * 3,
        check_vma=False,
    )
```

time: 368 us -> 194 us (0.53)
  the two profiles are of different devices: /device:TPU:440 before, /device:TPU:64 now
where the time goes in v1:
time: 194 us
  Pallas kernels  122 us (63%)
  waiting for transfers between devices  30.7 us (16%)
  blocking collectives  27.3 us (14%)
  starting transfers between devices  8.3 us (4%)
  local copies, waits for them, and re-layouts  2.9 us (1%)
    pallas_call x1, Pallas kernels, pack(): pl.pallas_call(pack_kernel, out_shape=jax.ShapeDtypeStruct((TEAM, IN_ROWS...  65.6 us
    pallas_call x1, Pallas kernels, unpack(): pl.pallas_call(unpack_kernel, out_shape=(shape,) * 3, in_specs=[anywhere]...  49 us
    all_to_all x1, waiting for transfers between devices, body(): messages = lax.all_to_all(packed, team, 0, 0, tiled=True)  30.7 us
    all_to_all x1, blocking collectives, body(): grads = lax.all_to_all(attend(swap, docs, messages), team, 0, 0, tiled=True)  27.3 us
    all_to_all x1, starting transfers between devices, body(): messages = lax.all_to_all(packed, team, 0, 0, tiled=True)  8.3 us
    pallas_call x1, Pallas kernels, attend(): pl.pallas_call(attend_kernel, out_shape=jax.ShapeDtypeStruct((TEAM, OUT_R...  7.74 us
  transfers between devices with their start and end apart: 1, of which 1 were waited for; matrix products, arithmetic and copies ran while one was open for 1% of the time, Pallas kernels for 0%

profile of v1, /device:TPU:64, one launch (start us, length us, event | category | flops | bytes accessed | tf_op | source)
XLA Modules:
  0.0 193.8 jit_solution(15309215836731453123)
XLA Ops:
  0.6 65.6 %pack.1 = bf16[8,528,256]{2,1,0:T(8,128)(2,1)} custom-call(bf16[1,128,2048]{2,1,0:T(8,128)(2,1)} %q_ref.1, bf16[1,128,2048]{2,1,0:T(8,128)(2,1)} %k_ref.1, bf16[1,128,2048]{2,1,0:T(8,128)(2,1)} %v_ref.1, bf16[1,128,2048]{2,1,0:T(8,128)(2,1)} %g_ref.1, bf16[16,128]{1,0:T(8,128)(2,1)} %bitcast.12, bf16[16,128]{1,0:T(8,128)(2,1)} %bitcast.13), custom_call_target="tpu_custom_call" | custom-call | tf_op jit(solution)/shard_map/pack/pallas_call | solution.py:58
  66.3 0.0 copy-start.1
  66.3 8.3 %all-to-all-start = ((bf16[8,528,256]{2,1,0:T(8,128)(2,1)}), bf16[8,528,256]{2,1,0:T(8,128)(2,1)S(1)}, u32[]{:S(2)}, u32[]{:S(2)}) async-start(bf16[8,528,256]{2,1,0:T(8,128)(2,1)} %pack.1), calls=%async_computation | async-start | bytes 4325376 | tf_op jit(solution)/shard_map/all_to_all | solution.py:173
  74.6 1.3 dynamic_slice.6
  76.5 0.0 copy-done.1
  76.5 0.1 reshape.13
  76.6 0.1 constant_dynamic-slice_fusion
  76.7 0.1 copy.13
  76.8 0.2 reduce_window_sum.14
  77.0 0.7 convert_reduce_fusion.docs_ref
  77.7 30.7 %all-to-all-done.in_ref = bf16[8,528,256]{2,1,0:T(8,128)(2,1)S(1)} async-done(((bf16[8,528,256]{2,1,0:T(8,128)(2,1)}), bf16[8,528,256]{2,1,0:T(8,128)(2,1)S(1)}, u32[]{:S(2)}, u32[]{:S(2)}) %all-to-all-start) | async-done | bytes 2162720 | tf_op jit(solution)/shard_map/all_to_all | solution.py:173
  108.4 0.0 copy-start
  108.4 1.3 copy-done
  109.8 7.7 %attend.1 = bf16[8,384,256]{2,1,0:T(8,128)(2,1)} custom-call(s32[1]{0:T(128)} %bitcast.1.swap_ref, s32[2,4]{1,0:T(2,128)} %convert_reduce_fusion.docs_ref, bf16[8,528,256]{2,1,0:T(8,128)(2,1)} %copy-done), custom_call_target="tpu_custom_call" | custom-call | tf_op jit(solution)/shard_map/attend/pallas_call | solution.py:112
  117.5 27.3 %all_to_all.10.in_ref = bf16[8,384,256]{2,1,0:T(8,128)(2,1)} all-to-all(bf16[8,384,256]{2,1,0:T(8,128)(2,1)} %attend.1), channel_id=1, replica_groups=mesh['side'=2,'low'=8,'bin'=8,'spot'=4] {'side','spot'}, dimensions={0} | all-to-all | bytes 3145728 | tf_op jit(solution)/shard_map/all_to_all | solution.py:174
  144.8 49.0 %unpack.1 = (bf16[1,128,2048]{2,1,0:T(8,128)(2,1)}, bf16[1,128,2048]{2,1,0:T(8,128)(2,1)}, bf16[1,128,2048]{2,1,0:T(8,128)(2,1)}) custom-call(bf16[8,384,256]{2,1,0:T(8,128)(2,1)} %all_to_all.10.in_ref), custom_call_target="tpu_custom_call" | custom-call | tf_op jit(solution)/shard_map/unpack/pallas_call | solution.py:150
Async XLA Ops:
  66.3 10.2 %copy-start.1 = (s32[16,8,4]{0,2,1:T(4,128)S(1)}, s32[16,8,4]{0,2,1:T(4,128)}, u32[]{:S(2)}) copy-start(s32[16,8,4]{0,2,1:T(4,128)} %param.14) | copy-start | bytes 6148
  66.3 42.1 %all-to-all-start = ((bf16[8,528,256]{2,1,0:T(8,128)(2,1)}), bf16[8,528,256]{2,1,0:T(8,128)(2,1)S(1)}, u32[]{:S(2)}, u32[]{:S(2)}) async-start(bf16[8,528,256]{2,1,0:T(8,128)(2,1)} %pack.1), calls=%async_computation | async-start | bytes 4325376 | tf_op jit(solution)/shard_map/all_to_all | solution.py:173
  108.4 1.4 copy-start

commit v2 on v1

--- a/solution.py
+++ b/solution.py
@@ -1,4 +1,3 @@
-import functools
 import math
 
 import jax
@@ -17,54 +16,46 @@
 STAT_ROWS = 16
 IN_ROWS = 4 * TOK + STAT_ROWS
 OUT_ROWS = 3 * TOK
+PACK_STEPS = 4
 MASKED = -1e30
 ROOT = 1.0 / math.sqrt(HEAD)
 LOG2E = math.log2(math.e)
 
 
-def pack_kernel(q_ref, k_ref, v_ref, g_ref, norm_ref, delta_ref, out_ref, stats, sems, stat_sem):
-    width = out_ref.shape[2]
-    copies = []
-    for member in range(TEAM):
-        for slot, ref in enumerate((q_ref, k_ref, v_ref, g_ref)):
-            copy = pltpu.make_async_copy(
-                ref.at[0, :, pl.ds(member * width, width)],
-                out_ref.at[member, pl.ds(slot * TOK, TOK), :],
-                sems.at[member, slot],
-            )
-            copy.start()
-            copies.append(copy)
-    heads = norm_ref.shape[0]
+def pack_kernel(q_ref, k_ref, v_ref, g_ref, norm_ref, delta_ref, out_ref):
+    members, _, width = out_ref.shape
+    step = pl.program_id(0)
+    row = lax.broadcasted_iota(jnp.int32, (STAT_ROWS, HEAD), 0)
+    per_member = width // HEAD
     norm = norm_ref[...].astype(jnp.float32)
     delta = delta_ref[...].astype(jnp.float32)
-    row = lax.broadcasted_iota(jnp.int32, (STAT_ROWS, HEAD), 0)
-    per_member = heads // TEAM
-    for head in range(heads):
-        tile = jnp.where(row == 0, norm[head : head + 1], 0.0)
-        tile = jnp.where(row == 1, delta[head : head + 1], tile)
-        place = head % per_member * HEAD
-        stats[head // per_member, :, place : place + HEAD] = tile.astype(jnp.bfloat16)
-    copy = pltpu.make_async_copy(stats, out_ref.at[:, pl.ds(4 * TOK, STAT_ROWS), :], stat_sem)
-    copy.start()
-    copies.append(copy)
-    for copy in copies:
-        copy.wait()
+    head_row = lax.broadcasted_iota(jnp.int32, norm.shape, 0)
+    for member in range(members):
+        for slot, ref in enumerate((q_ref, k_ref, v_ref, g_ref)):
+            out_ref[member, slot * TOK : (slot + 1) * TOK, :] = ref[
+                0, :, member * width : (member + 1) * width
+            ]
+        for place in range(per_member):
+            here = head_row == (step * members + member) * per_member + place
+            head_norm = jnp.sum(jnp.where(here, norm, 0.0), axis=0, keepdims=True)
+            head_delta = jnp.sum(jnp.where(here, delta, 0.0), axis=0, keepdims=True)
+            tile = jnp.where(row == 0, head_norm, jnp.where(row == 1, head_delta, 0.0))
+            out_ref[member, 4 * TOK :, place * HEAD : (place + 1) * HEAD] = tile.astype(
+                jnp.bfloat16
+            )
 
 
 def pack(q, k, v, g, norm, delta):
     width = q.shape[2] // TEAM
-    anywhere = pl.BlockSpec(memory_space=pl.ANY)
-    local = pl.BlockSpec(memory_space=pltpu.VMEM)
+    members = TEAM // PACK_STEPS
+    columns = pl.BlockSpec((1, TOK, members * width), lambda step: (0, 0, step))
+    stats = pl.BlockSpec(norm.shape, lambda step: (0, 0))
     return pl.pallas_call(
         pack_kernel,
         out_shape=jax.ShapeDtypeStruct((TEAM, IN_ROWS, width), jnp.bfloat16),
-        in_specs=[anywhere] * 4 + [local] * 2,
-        out_specs=anywhere,
-        scratch_shapes=[
-            pltpu.VMEM((TEAM, STAT_ROWS, width), jnp.bfloat16),
-            pltpu.SemaphoreType.DMA((TEAM, 4)),
-            pltpu.SemaphoreType.DMA,
-        ],
+        grid=(PACK_STEPS,),
+        in_specs=[columns] * 4 + [stats] * 2,
+        out_specs=pl.BlockSpec((members, IN_ROWS, width), lambda step: (step, 0, 0)),
         name="pack",
     )(q, k, v, g, norm, delta)
 
@@ -128,31 +119,25 @@
     )(swap, docs, messages)
 
 
-def unpack_kernel(in_ref, q_ref, k_ref, v_ref, sems):
-    width = in_ref.shape[2]
-    copies = []
-    for member in range(TEAM):
+def unpack_kernel(in_ref, q_ref, k_ref, v_ref):
+    members, _, width = in_ref.shape
+    for member in range(members):
         for slot, ref in enumerate((q_ref, k_ref, v_ref)):
-            copy = pltpu.make_async_copy(
-                in_ref.at[member, pl.ds(slot * TOK, TOK), :],
-                ref.at[0, :, pl.ds(member * width, width)],
-                sems.at[member, slot],
-            )
-            copy.start()
-            copies.append(copy)
-    for copy in copies:
-        copy.wait()
+            ref[0, :, member * width : (member + 1) * width] = in_ref[
+                member, slot * TOK : (slot + 1) * TOK, :
+            ]
 
 
 def unpack(messages):
-    anywhere = pl.BlockSpec(memory_space=pl.ANY)
-    shape = jax.ShapeDtypeStruct((1, TOK, TEAM * messages.shape[2]), jnp.bfloat16)
+    width = messages.shape[2]
+    members = TEAM // PACK_STEPS
+    columns = pl.BlockSpec((1, TOK, members * width), lambda step: (0, 0, step))
     return pl.pallas_call(
         unpack_kernel,
-        out_shape=(shape,) * 3,
-        in_specs=[anywhere],
-        out_specs=(anywhere,) * 3,
-        scratch_shapes=[pltpu.SemaphoreType.DMA((TEAM, 3))],
+        out_shape=(jax.ShapeDtypeStruct((1, TOK, TEAM * width), jnp.bfloat16),) * 3,
+        grid=(PACK_STEPS,),
+        in_specs=[pl.BlockSpec((members, OUT_ROWS, width), lambda step: (step, 0, 0))],
+        out_specs=(columns,) * 3,
         name="unpack",
     )(messages)
 

time: 194 us -> 87.2 us (0.45)
  the two profiles are of different devices: /device:TPU:64 before, /device:TPU:128 now
where the time goes in v2:
time: 87.2 us; the launch traced here: 86.7 us
  waiting for transfers between devices  30.7 us (35%)
  blocking collectives  27.3 us (31%)
  Pallas kernels  15.1 us (17%)
  starting transfers between devices  8.42 us (10%)
  local copies, waits for them, and re-layouts  2.9 us (3%)
  between operations  1.3 us (1%)
  other arithmetic  0.9 us (1%)
    all_to_all x1, waiting for transfers between devices, body(): messages = lax.all_to_all(packed, team, 0, 0, tiled=True)  30.7 us
    all_to_all x1, blocking collectives, body(): grads = lax.all_to_all(attend(swap, docs, messages), team, 0, 0, tiled=True)  27.3 us
    all_to_all x1, starting transfers between devices, body(): messages = lax.all_to_all(packed, team, 0, 0, tiled=True)  8.42 us
    pallas_call x1, Pallas kernels, attend(): pl.pallas_call(attend_kernel, out_shape=jax.ShapeDtypeStruct((TEAM, OUT_R...  7.73 us
    pallas_call x1, Pallas kernels, pack(): pl.pallas_call(pack_kernel, out_shape=jax.ShapeDtypeStruct((TEAM, IN_ROWS...  3.84 us
    pallas_call x1, Pallas kernels, unpack(): pl.pallas_call(unpack_kernel, out_shape=(jax.ShapeDtypeStruct((1, TOK, TE...  3.55 us
  transfers between devices with their start and end apart: 1, of which 1 were waited for; matrix products, arithmetic and copies ran while one was open for 3% of the time, Pallas kernels for 0%

profile of v2, /device:TPU:128, one launch (start us, length us, event | category | flops | bytes accessed | tf_op | source)
XLA Modules:
  0.0 86.7 jit_solution(3838403220902503087)
XLA Ops:
  0.6 3.8 %pack.1 = bf16[8,528,256]{2,1,0:T(8,128)(2,1)} custom-call(bf16[1,128,2048]{2,1,0:T(8,128)(2,1)} %q_ref.1, bf16[1,128,2048]{2,1,0:T(8,128)(2,1)} %k_ref.1, bf16[1,128,2048]{2,1,0:T(8,128)(2,1)} %v_ref.1, bf16[1,128,2048]{2,1,0:T(8,128)(2,1)} %g_ref.1, bf16[16,128]{1,0:T(8,128)(2,1)} %bitcast.12, bf16[16,128]{1,0:T(8,128)(2,1)} %bitcast.13), custom_call_target="tpu_custom_call" | custom-call | tf_op jit(solution)/shard_map/pack/pallas_call | solution.py:53
  4.5 0.0 copy-start.1
  4.5 8.4 %all-to-all-start = ((bf16[8,528,256]{2,1,0:T(8,128)(2,1)}), bf16[8,528,256]{2,1,0:T(8,128)(2,1)S(1)}, u32[]{:S(2)}, u32[]{:S(2)}) async-start(bf16[8,528,256]{2,1,0:T(8,128)(2,1)} %pack.1), calls=%async_computation | async-start | bytes 4325376 | tf_op jit(solution)/shard_map/all_to_all | solution.py:158
  12.9 1.3 %dynamic_slice.6 = s32[1,1]{0,1:T(1,128)} dynamic-slice(s32[16,8]{0,1:T(8,128)} %param.15, s32[]{:T(128)S(6)} %select_n.10, s32[]{:T(128)S(6)} %select_n.11), dynamic_slice_sizes={1,1} | dynamic-slice | bytes 12 | tf_op jit(solution)/shard_map/dynamic_slice | solution.py:149
  14.8 0.0 copy-done.1
  14.8 0.1 reshape.13
  14.9 0.1 constant_dynamic-slice_fusion
  15.0 0.1 copy.13
  15.1 0.2 reduce_window_sum.14
  15.3 0.7 convert_reduce_fusion.docs_ref
  16.0 30.7 %all-to-all-done.in_ref = bf16[8,528,256]{2,1,0:T(8,128)(2,1)S(1)} async-done(((bf16[8,528,256]{2,1,0:T(8,128)(2,1)}), bf16[8,528,256]{2,1,0:T(8,128)(2,1)S(1)}, u32[]{:S(2)}, u32[]{:S(2)}) %all-to-all-start) | async-done | bytes 2162720 | tf_op jit(solution)/shard_map/all_to_all | solution.py:158
  46.7 0.0 copy-start
  46.7 1.3 %copy-done = bf16[8,528,256]{2,1,0:T(8,128)(2,1)} copy-done((bf16[8,528,256]{2,1,0:T(8,128)(2,1)}, bf16[8,528,256]{2,1,0:T(8,128)(2,1)S(1)}, u32[]{:S(2)}) %copy-start) | copy-done | bytes 2162712
  48.1 7.7 %attend.1 = bf16[8,384,256]{2,1,0:T(8,128)(2,1)} custom-call(s32[1]{0:T(128)} %bitcast.1.swap_ref, s32[2,4]{1,0:T(2,128)} %convert_reduce_fusion.docs_ref, bf16[8,528,256]{2,1,0:T(8,128)(2,1)} %copy-done), custom_call_target="tpu_custom_call" | custom-call | tf_op jit(solution)/shard_map/attend/pallas_call | solution.py:103
  55.8 27.3 %all_to_all.10.in_ref = bf16[8,384,256]{2,1,0:T(8,128)(2,1)} all-to-all(bf16[8,384,256]{2,1,0:T(8,128)(2,1)} %attend.1), channel_id=1, replica_groups=mesh['side'=2,'low'=8,'bin'=8,'spot'=4] {'side','spot'}, dimensions={0} | all-to-all | bytes 3145728 | tf_op jit(solution)/shard_map/all_to_all | solution.py:159
  83.1 3.6 %unpack.1 = (bf16[1,128,2048]{2,1,0:T(8,128)(2,1)}, bf16[1,128,2048]{2,1,0:T(8,128)(2,1)}, bf16[1,128,2048]{2,1,0:T(8,128)(2,1)}) custom-call(bf16[8,384,256]{2,1,0:T(8,128)(2,1)} %all_to_all.10.in_ref), custom_call_target="tpu_custom_call" | custom-call | tf_op jit(solution)/shard_map/unpack/pallas_call | solution.py:135
Async XLA Ops:
  4.5 10.3 %copy-start.1 = (s32[16,8,4]{0,2,1:T(4,128)S(1)}, s32[16,8,4]{0,2,1:T(4,128)}, u32[]{:S(2)}) copy-start(s32[16,8,4]{0,2,1:T(4,128)} %param.14) | copy-start | bytes 6148
  4.5 42.3 %all-to-all-start = ((bf16[8,528,256]{2,1,0:T(8,128)(2,1)}), bf16[8,528,256]{2,1,0:T(8,128)(2,1)S(1)}, u32[]{:S(2)}, u32[]{:S(2)}) async-start(bf16[8,528,256]{2,1,0:T(8,128)(2,1)} %pack.1), calls=%async_computation | async-start | bytes 4325376 | tf_op jit(solution)/shard_map/all_to_all | solution.py:158
  46.7 1.4 %copy-start = (bf16[8,528,256]{2,1,0:T(8,128)(2,1)}, bf16[8,528,256]{2,1,0:T(8,128)(2,1)S(1)}, u32[]{:S(2)}) copy-start(bf16[8,528,256]{2,1,0:T(8,128)(2,1)S(1)} %all-to-all-done.in_ref) | copy-start | bytes 6488068

commit v3 on v1

v3 whole, which is shorter than its diff:
```python
import math

import jax
import jax.numpy as jnp
from jax import lax
from jax.experimental import pallas as pl
from jax.experimental.pallas import tpu as pltpu
from jax.sharding import Mesh
from jax.sharding import PartitionSpec as P

TOK = 128
HEAD = 128
SIDES = 2
SPOTS = 4
TEAM = SIDES * SPOTS
STAT_ROWS = 16
IN_ROWS = 4 * TOK + STAT_ROWS
OUT_ROWS = 3 * TOK
MASKED = -1e30
ROOT = 1.0 / math.sqrt(HEAD)
LOG2E = math.log2(math.e)
VMEM_LIMIT = 24 << 20


def start_all(copies):
    for copy in copies:
        copy.start()
    return copies


def pack_kernel(q_ref, k_ref, v_ref, g_ref, norm_ref, delta_ref, out_ref, stats, sems, stat_sems):
    width = out_ref.shape[2]
    stat_copies = start_all(
        [
            pltpu.make_async_copy(ref, stats.at[slot], stat_sems.at[slot])
            for slot, ref in enumerate((norm_ref, delta_ref))
        ]
    )
    copies = start_all(
        [
            pltpu.make_async_copy(
                ref.at[0, :, pl.ds(member * width, width)],
                out_ref.at[member, pl.ds(slot * TOK, TOK), :],
                sems.at[member, slot],
            )
            for member in range(TEAM)
            for slot, ref in enumerate((q_ref, k_ref, v_ref, g_ref))
        ]
    )
    for copy in stat_copies:
        copy.wait()
    norm = stats[0].astype(jnp.float32)
    delta = stats[1].astype(jnp.float32)
    row = lax.broadcasted_iota(jnp.int32, (STAT_ROWS, HEAD), 0)
    per_member = width // HEAD
    for head in range(TEAM * per_member):
        tile = jnp.where(row == 0, norm[head : head + 1], 0.0)
        tile = jnp.where(row == 1, delta[head : head + 1], tile)
        place = head % per_member * HEAD
        out_ref[head // per_member, 4 * TOK :, place : place + HEAD] = tile.astype(jnp.bfloat16)
    for copy in copies:
        copy.wait()


def in_hbm(array):
    return pltpu.with_memory_space_constraint(array, pltpu.HBM)


def in_vmem(array):
    return pltpu.with_memory_space_constraint(array, pltpu.VMEM)


ANYWHERE = pl.BlockSpec(memory_space=pl.ANY)
LOCAL = pl.BlockSpec(memory_space=pltpu.VMEM)
PARAMS = pltpu.CompilerParams(vmem_limit_bytes=VMEM_LIMIT)


def pack(q, k, v, g, norm, delta):
    width = q.shape[2] // TEAM
    return pl.pallas_call(
        pack_kernel,
        out_shape=pltpu.VMEM((TEAM, IN_ROWS, width), jnp.bfloat16),
        in_specs=[ANYWHERE] * 6,
        out_specs=LOCAL,
        scratch_shapes=[
            pltpu.VMEM((2,) + norm.shape, jnp.bfloat16),
            pltpu.SemaphoreType.DMA((TEAM, 4)),
            pltpu.SemaphoreType.DMA((2,)),
        ],
        compiler_params=PARAMS,
        name="pack",
    )(*(in_hbm(array) for array in (q, k, v, g, norm, delta)))


def nt(a, b):
    return lax.dot_general(a, b, (((1,), (1,)), ((), ())), preferred_element_type=jnp.float32)


def nn(a, b):
    return jnp.dot(a, b, preferred_element_type=jnp.float32)


def attend_kernel(swap_ref, docs_ref, in_ref, out_ref, ds_ref):
    span = SPOTS * TOK
    per_member = in_ref.shape[2] // HEAD
    swap = swap_ref[0]

    @pl.loop(0, SIDES * per_member)
    def unit(index):
        side = index // per_member
        lanes = pl.ds(pl.multiple_of(index % per_member * HEAD, HEAD), HEAD)
        source = pl.ds(side * SPOTS, SPOTS)
        target = jnp.bitwise_xor(side, swap) * SPOTS

        def whole(slot):
            return in_ref[source, slot * TOK : (slot + 1) * TOK, lanes].reshape(span, HEAD)

        q, k, v, g = (whole(slot) for slot in range(4))
        stats = [
            in_ref[side * SPOTS + spot, 4 * TOK :, lanes].astype(jnp.float32)
            for spot in range(SPOTS)
        ]
        delta = jnp.concatenate([stat[1:2] for stat in stats], axis=1)
        for key_spot in range(SPOTS):
            rows = slice(key_spot * TOK, (key_spot + 1) * TOK)
            key_doc = docs_ref[side, key_spot]
            bias = jnp.concatenate(
                [
                    jnp.where(docs_ref[side, spot] == key_doc, stats[spot][0:1] * -LOG2E, MASKED)
                    for spot in range(SPOTS)
                ],
                axis=1,
            )
            probs = jnp.exp2(nt(k[rows], q) * (ROOT * LOG2E) + bias)
            dscores = (probs * (nt(v[rows], g) - delta)).astype(jnp.bfloat16)
            ds_ref[rows, :] = dscores
            out_ref[target + key_spot, TOK : 2 * TOK, lanes] = (nn(dscores, q) * ROOT).astype(
                jnp.bfloat16
            )
            out_ref[target + key_spot, 2 * TOK :, lanes] = nn(probs.astype(jnp.bfloat16), g).astype(
                jnp.bfloat16
            )
        dq = (nn(k.T, ds_ref[...]) * ROOT).T.astype(jnp.bfloat16)
        for spot in range(SPOTS):
            out_ref[target + spot, :TOK, lanes] = dq[spot * TOK : (spot + 1) * TOK]


def attend(swap, docs, messages):
    span = SPOTS * TOK
    units = SIDES * messages.shape[2] // HEAD
    scalars = pl.BlockSpec(memory_space=pltpu.SMEM)
    return pl.pallas_call(
        attend_kernel,
        out_shape=pltpu.VMEM((TEAM, OUT_ROWS, messages.shape[2]), jnp.bfloat16),
        in_specs=[scalars, scalars, LOCAL],
        out_specs=LOCAL,
        scratch_shapes=[pltpu.VMEM((span, span), jnp.bfloat16)],
        compiler_params=PARAMS,
        cost_estimate=pl.CostEstimate(
            flops=units * 10 * span * span * HEAD,
            bytes_accessed=4 << 20,
            transcendentals=units * span * span,
        ),
        name="attend",
    )(swap, docs, in_vmem(messages))


def unpack_kernel(in_ref, q_ref, k_ref, v_ref, sems):
    width = in_ref.shape[2]
    copies = start_all(
        [
            pltpu.make_async_copy(
                in_ref.at[member, pl.ds(slot * TOK, TOK), :],
                ref.at[0, :, pl.ds(member * width, width)],
                sems.at[member, slot],
            )
            for member in range(TEAM)
            for slot, ref in enumerate((q_ref, k_ref, v_ref))
        ]
    )
    for copy in copies:
        copy.wait()


def unpack(messages):
    shape = (1, TOK, TEAM * messages.shape[2])
    return pl.pallas_call(
        unpack_kernel,
        out_shape=(pltpu.HBM(shape, jnp.bfloat16),) * 3,
        in_specs=[LOCAL],
        out_specs=(ANYWHERE,) * 3,
        scratch_shapes=[pltpu.SemaphoreType.DMA((TEAM, 3))],
        compiler_params=PARAMS,
        name="unpack",
    )(in_vmem(messages))


def body(q, k, v, g, norm, delta, doc_lengths, bin_dest):
    groups = lax.axis_size("low")
    low = lax.axis_index("low")
    bin_index = lax.axis_index("bin")
    swap = (bin_dest[low, bin_index] != low).astype(jnp.int32)[None]
    lengths = doc_lengths.reshape((SIDES, groups) + doc_lengths.shape[1:])[:, low, bin_index]
    ends = jnp.cumsum(lengths, axis=1)
    docs = jnp.sum(
        (ends[:, None, :] <= jnp.arange(SPOTS, dtype=jnp.int32)[None, :, None]).astype(jnp.int32),
        axis=2,
    )
    team = ("side", "spot")
    packed = pack(q, k, v, g, jnp.transpose(norm[0]), jnp.transpose(delta[0]))
    messages = lax.all_to_all(packed, team, 0, 0, tiled=True)
    grads = lax.all_to_all(attend(swap, docs, messages), team, 0, 0, tiled=True)
    return unpack(grads)


def solution(mesh):
    dp, ctx = mesh.devices.shape
    fine = Mesh(
        mesh.devices.reshape(SIDES, dp // SIDES, ctx // SPOTS, SPOTS),
        ("side", "low", "bin", "spot"),
    )
    split = P(("side", "low"), ("bin", "spot"), None)
    return jax.shard_map(
        body,
        mesh=fine,
        in_specs=(split,) * 6 + (P(), P()),
        out_specs=(split,) * 3,
        check_vma=False,
    )
```

time: 194 us -> 80.3 us (0.41)
  the two profiles are of different devices: /device:TPU:64 before, /device:TPU:128 now
where the time goes in v3:
time: 80.3 us; the launch traced here: 79.9 us
  waiting for transfers between devices  31.3 us (39%)
  blocking collectives  26.9 us (33%)
  Pallas kernels  10.2 us (13%)
  starting transfers between devices  8.3 us (10%)
  local copies, waits for them, and re-layouts  1.55 us (2%)
  between operations  1.32 us (2%)
    all_to_all x1, waiting for transfers between devices, body(): messages = lax.all_to_all(packed, team, 0, 0, tiled=True)  31.3 us
    all_to_all x1, blocking collectives, body(): grads = lax.all_to_all(attend(swap, docs, messages), team, 0, 0, tiled=True)  26.9 us
    all_to_all x1, starting transfers between devices, body(): messages = lax.all_to_all(packed, team, 0, 0, tiled=True)  8.3 us
    pallas_call x1, Pallas kernels, attend(): pl.pallas_call(attend_kernel, out_shape=pltpu.VMEM((TEAM, OUT_ROWS, messa...  5.67 us
    pallas_call x1, Pallas kernels, pack(): pl.pallas_call(pack_kernel, out_shape=pltpu.VMEM((TEAM, IN_ROWS, width),...  3.24 us
  transfers between devices with their start and end apart: 1, of which 1 were waited for; matrix products, arithmetic and copies ran while one was open for 2% of the time, Pallas kernels for 0%

profile of v3, /device:TPU:128, one launch (start us, length us, event | category | flops | bytes accessed | tf_op | source)
XLA Modules:
  0.0 79.9 jit_solution(12162613244039759810)
XLA Ops:
  0.6 3.2 %pack.1 = bf16[8,528,256]{2,1,0:T(8,128)(2,1)} custom-call(bf16[1,128,2048]{2,1,0:T(8,128)(2,1)} %q_ref.1, bf16[1,128,2048]{2,1,0:T(8,128)(2,1)} %k_ref.1, bf16[1,128,2048]{2,1,0:T(8,128)(2,1)} %v_ref.1, bf16[1,128,2048]{2,1,0:T(8,128)(2,1)} %g_ref.1, bf16[16,128]{1,0:T(8,128)(2,1)} %bitcast.12, bf16[16,128]{1,0:T(8,128)(2,1)} %bitcast.13), custom_call_target="tpu_custom_call" | custom-call | tf_op jit(solution)/shard_map/pack/pallas_call | solution.py:80
  3.9 0.0 copy-start
  3.9 8.3 %all-to-all-start = ((bf16[8,528,256]{2,1,0:T(8,128)(2,1)}), bf16[8,528,256]{2,1,0:T(8,128)(2,1)S(1)}, u32[]{:S(2)}, u32[]{:S(2)}) async-start(bf16[8,528,256]{2,1,0:T(8,128)(2,1)} %pack.1), calls=%async_computation | async-start | bytes 4325376 | tf_op jit(solution)/shard_map/all_to_all | solution.py:211
  12.2 1.3 %dynamic_slice.6 = s32[1,1]{0,1:T(1,128)} dynamic-slice(s32[16,8]{0,1:T(8,128)} %param.15, s32[]{:T(128)S(6)} %select_n.10, s32[]{:T(128)S(6)} %select_n.11), dynamic_slice_sizes={1,1} | dynamic-slice | bytes 12 | tf_op jit(solution)/shard_map/dynamic_slice | solution.py:202
  14.1 0.0 copy-done
  14.1 0.1 reshape.13
  14.2 0.1 constant_dynamic-slice_fusion
  14.3 0.1 copy.13
  14.4 0.2 reduce_window_sum.14
  14.6 0.1 convert_reduce_fusion.docs_ref
  14.7 31.3 %all-to-all-done.in_ref = bf16[8,528,256]{2,1,0:T(8,128)(2,1)S(1)} async-done(((bf16[8,528,256]{2,1,0:T(8,128)(2,1)}), bf16[8,528,256]{2,1,0:T(8,128)(2,1)S(1)}, u32[]{:S(2)}, u32[]{:S(2)}) %all-to-all-start) | async-done | bytes 2162720 | tf_op jit(solution)/shard_map/all_to_all | solution.py:211
  46.0 5.7 %attend.1 = bf16[8,384,256]{2,1,0:T(8,128)(2,1)S(1)} custom-call(s32[1]{0:T(128)} %bitcast.1.swap_ref, s32[2,4]{1,0:T(2,128)S(1)} %convert_reduce_fusion.docs_ref, bf16[8,528,256]{2,1,0:T(8,128)(2,1)S(1)} %all-to-all-done.in_ref), custom_call_target="tpu_custom_call" | custom-call | flops 1342177280 | bytes 4194304 | tf_op jit(solution)/shard_map/attend/pallas_call | solution.py:152
  51.7 26.9 %all_to_all.10.in_ref = bf16[8,384,256]{2,1,0:T(8,128)(2,1)S(1)} all-to-all(bf16[8,384,256]{2,1,0:T(8,128)(2,1)S(1)} %attend.1), channel_id=1, replica_groups=mesh['side'=2,'low'=8,'bin'=8,'spot'=4] {'side','spot'}, dimensions={0} | all-to-all | bytes 3145728 | tf_op jit(solution)/shard_map/all_to_all | solution.py:212
  78.6 1.3 %unpack.1 = (bf16[1,128,2048]{2,1,0:T(8,128)(2,1)}, bf16[1,128,2048]{2,1,0:T(8,128)(2,1)}, bf16[1,128,2048]{2,1,0:T(8,128)(2,1)}) custom-call(bf16[8,384,256]{2,1,0:T(8,128)(2,1)S(1)} %all_to_all.10.in_ref), custom_call_target="tpu_custom_call" | custom-call | tf_op jit(solution)/shard_map/unpack/pallas_call | solution.py:187
Async XLA Ops:
  3.9 10.2 %copy-start = (s32[16,8,4]{0,2,1:T(4,128)S(1)}, s32[16,8,4]{0,2,1:T(4,128)}, u32[]{:S(2)}) copy-start(s32[16,8,4]{0,2,1:T(4,128)} %param.14) | copy-start | bytes 6148
  3.9 42.1 %all-to-all-start = ((bf16[8,528,256]{2,1,0:T(8,128)(2,1)}), bf16[8,528,256]{2,1,0:T(8,128)(2,1)S(1)}, u32[]{:S(2)}, u32[]{:S(2)}) async-start(bf16[8,528,256]{2,1,0:T(8,128)(2,1)} %pack.1), calls=%async_computation | async-start | bytes 4325376 | tf_op jit(solution)/shard_map/all_to_all | solution.py:211

commit v4 on v3

--- a/solution.py
+++ b/solution.py
@@ -19,6 +19,7 @@
 MASKED = -1e30
 ROOT = 1.0 / math.sqrt(HEAD)
 LOG2E = math.log2(math.e)
+QUERY_SPOTS = 4
 VMEM_LIMIT = 24 << 20
 
 
@@ -28,7 +29,7 @@
     return copies
 
 
-def pack_kernel(q_ref, k_ref, v_ref, g_ref, norm_ref, delta_ref, out_ref, stats, sems, stat_sems):
+def pack_kernel(q_ref, k_ref, v_ref, g_ref, norm_ref, delta_ref, out_ref, held, stats, sems, stat_sems):
     width = out_ref.shape[2]
     stat_copies = start_all(
         [
@@ -38,12 +39,7 @@
     )
     copies = start_all(
         [
-            pltpu.make_async_copy(
-                ref.at[0, :, pl.ds(member * width, width)],
-                out_ref.at[member, pl.ds(slot * TOK, TOK), :],
-                sems.at[member, slot],
-            )
-            for member in range(TEAM)
+            pltpu.make_async_copy(ref.at[0], held.at[slot], sems.at[slot])
             for slot, ref in enumerate((q_ref, k_ref, v_ref, g_ref))
         ]
     )
@@ -58,8 +54,12 @@
         tile = jnp.where(row == 1, delta[head : head + 1], tile)
         place = head % per_member * HEAD
         out_ref[head // per_member, 4 * TOK :, place : place + HEAD] = tile.astype(jnp.bfloat16)
-    for copy in copies:
+    for slot, copy in enumerate(copies):
         copy.wait()
+        for member in range(TEAM):
+            out_ref[member, slot * TOK : (slot + 1) * TOK, :] = held[
+                slot, :, member * width : (member + 1) * width
+            ]
 
 
 def in_hbm(array):
@@ -83,8 +83,9 @@
         in_specs=[ANYWHERE] * 6,
         out_specs=LOCAL,
         scratch_shapes=[
+            pltpu.VMEM((4,) + q.shape[1:], jnp.bfloat16),
             pltpu.VMEM((2,) + norm.shape, jnp.bfloat16),
-            pltpu.SemaphoreType.DMA((TEAM, 4)),
+            pltpu.SemaphoreType.DMA((4,)),
             pltpu.SemaphoreType.DMA((2,)),
         ],
         compiler_params=PARAMS,
@@ -100,49 +101,63 @@
     return jnp.dot(a, b, preferred_element_type=jnp.float32)
 
 
-def attend_kernel(swap_ref, docs_ref, in_ref, out_ref, ds_ref):
+def attend_kernel(swap_ref, docs_ref, in_ref, out_ref):
     span = SPOTS * TOK
     per_member = in_ref.shape[2] // HEAD
     swap = swap_ref[0]
 
-    @pl.loop(0, SIDES * per_member)
-    def unit(index):
-        side = index // per_member
-        lanes = pl.ds(pl.multiple_of(index % per_member * HEAD, HEAD), HEAD)
-        source = pl.ds(side * SPOTS, SPOTS)
+    def unit(side, lanes):
+        source = slice(side * SPOTS, (side + 1) * SPOTS)
         target = jnp.bitwise_xor(side, swap) * SPOTS
 
         def whole(slot):
             return in_ref[source, slot * TOK : (slot + 1) * TOK, lanes].reshape(span, HEAD)
 
         q, k, v, g = (whole(slot) for slot in range(4))
-        stats = [
-            in_ref[side * SPOTS + spot, 4 * TOK :, lanes].astype(jnp.float32)
-            for spot in range(SPOTS)
-        ]
-        delta = jnp.concatenate([stat[1:2] for stat in stats], axis=1)
-        for key_spot in range(SPOTS):
-            rows = slice(key_spot * TOK, (key_spot + 1) * TOK)
-            key_doc = docs_ref[side, key_spot]
-            bias = jnp.concatenate(
-                [
-                    jnp.where(docs_ref[side, spot] == key_doc, stats[spot][0:1] * -LOG2E, MASKED)
-                    for spot in range(SPOTS)
-                ],
-                axis=1,
-            )
-            probs = jnp.exp2(nt(k[rows], q) * (ROOT * LOG2E) + bias)
-            dscores = (probs * (nt(v[rows], g) - delta)).astype(jnp.bfloat16)
-            ds_ref[rows, :] = dscores
-            out_ref[target + key_spot, TOK : 2 * TOK, lanes] = (nn(dscores, q) * ROOT).astype(
-                jnp.bfloat16
-            )
-            out_ref[target + key_spot, 2 * TOK :, lanes] = nn(probs.astype(jnp.bfloat16), g).astype(
-                jnp.bfloat16
-            )
-        dq = (nn(k.T, ds_ref[...]) * ROOT).T.astype(jnp.bfloat16)
+        k_turned = k.T
+        dk = jnp.zeros((span, HEAD), jnp.float32)
+        dv = jnp.zeros((span, HEAD), jnp.float32)
+        for first in range(0, SPOTS, QUERY_SPOTS):
+            spots = range(first, first + QUERY_SPOTS)
+            columns = slice(first * TOK, (first + QUERY_SPOTS) * TOK)
+            stats = [
+                in_ref[side * SPOTS + spot, 4 * TOK :, lanes].astype(jnp.float32)
+                for spot in spots
+            ]
+            delta = jnp.concatenate([stat[1:2] for stat in stats], axis=1)
+            scores = nt(k, q[columns])
+            dprobs = nt(v, g[columns])
+            probs_low, dscores = [], []
+            for key_spot in range(SPOTS):
+                rows = slice(key_spot * TOK, (key_spot + 1) * TOK)
+                key_doc = docs_ref[side, key_spot]
+                bias = jnp.concatenate(
+                    [
+                        jnp.where(docs_ref[side, spot] == key_doc, stat[0:1] * -LOG2E, MASKED)
+                        for spot, stat in zip(spots, stats)
+                    ],
+                    axis=1,
+                )
+                probs = jnp.exp2(scores[rows] * (ROOT * LOG2E) + bias)
+                probs_low.append(probs.astype(jnp.bfloat16))
+                dscores.append((probs * (dprobs[rows] - delta)).astype(jnp.bfloat16))
+            probs_low = jnp.concatenate(probs_low, axis=0)
+            dscores = jnp.concatenate(dscores, axis=0)
+            dk = dk + nn(dscores, q[columns])
+            dv = dv + nn(probs_low, g[columns])
+            dq = (nn(k_turned, dscores) * ROOT).T.astype(jnp.bfloat16)
+            for place, spot in enumerate(spots):
+                out_ref[target + spot, :TOK, lanes] = dq[place * TOK : (place + 1) * TOK]
+        dk = (dk * ROOT).astype(jnp.bfloat16)
+        dv = dv.astype(jnp.bfloat16)
         for spot in range(SPOTS):
-            out_ref[target + spot, :TOK, lanes] = dq[spot * TOK : (spot + 1) * TOK]
+            rows = slice(spot * TOK, (spot + 1) * TOK)
+            out_ref[target + spot, TOK : 2 * TOK, lanes] = dk[rows]
+            out_ref[target + spot, 2 * TOK :, lanes] = dv[rows]
+
+    for side in range(SIDES):
+        for head in range(per_member):
+            unit(side, slice(head * HEAD, (head + 1) * HEAD))
 
 
 def attend(swap, docs, messages):
@@ -154,7 +169,6 @@
         out_shape=pltpu.VMEM((TEAM, OUT_ROWS, messages.shape[2]), jnp.bfloat16),
         in_specs=[scalars, scalars, LOCAL],
         out_specs=LOCAL,
-        scratch_shapes=[pltpu.VMEM((span, span), jnp.bfloat16)],
         compiler_params=PARAMS,
         cost_estimate=pl.CostEstimate(
             flops=units * 10 * span * span * HEAD,

time: 80.3 us -> 77.5 us (0.965)
  Pallas kernels: 10.2 us -> 7.55 us
    pallas_call x1, Pallas kernels: 5.67 us -> 3.24 us  [attend(): pl.pallas_call(attend_kernel, out_shape=pltpu.VMEM((TEAM, OUT_ROWS, messa...]
where the time goes in v4:
time: 77.5 us; the launch traced here: 77.2 us
  waiting for transfers between devices  31.3 us (40%)
  blocking collectives  26.9 us (35%)
  starting transfers between devices  8.3 us (11%)
  Pallas kernels  7.55 us (10%)
  local copies, waits for them, and re-layouts  1.55 us (2%)
  between operations  1.32 us (2%)
    all_to_all x1, waiting for transfers between devices, body(): messages = lax.all_to_all(packed, team, 0, 0, tiled=True)  31.3 us
    all_to_all x1, blocking collectives, body(): grads = lax.all_to_all(attend(swap, docs, messages), team, 0, 0, tiled=True)  26.9 us
    all_to_all x1, starting transfers between devices, body(): messages = lax.all_to_all(packed, team, 0, 0, tiled=True)  8.3 us
    pallas_call x1, Pallas kernels, attend(): pl.pallas_call(attend_kernel, out_shape=pltpu.VMEM((TEAM, OUT_ROWS, messa...  3.24 us
    pallas_call x1, Pallas kernels, pack(): pl.pallas_call(pack_kernel, out_shape=pltpu.VMEM((TEAM, IN_ROWS, width),...  2.99 us
  transfers between devices with their start and end apart: 1, of which 1 were waited for; matrix products, arithmetic and copies ran while one was open for 2% of the time, Pallas kernels for 0%

profile of v4, /device:TPU:128, one launch (start us, length us, event | category | flops | bytes accessed | tf_op | source)
XLA Modules:
  0.0 77.2 jit_solution(6948780586534506443)
XLA Ops:
  0.6 3.0 %pack.1 = bf16[8,528,256]{2,1,0:T(8,128)(2,1)} custom-call(bf16[1,128,2048]{2,1,0:T(8,128)(2,1)} %q_ref.1, bf16[1,128,2048]{2,1,0:T(8,128)(2,1)} %k_ref.1, bf16[1,128,2048]{2,1,0:T(8,128)(2,1)} %v_ref.1, bf16[1,128,2048]{2,1,0:T(8,128)(2,1)} %g_ref.1, bf16[16,128]{1,0:T(8,128)(2,1)} %bitcast.12, bf16[16,128]{1,0:T(8,128)(2,1)} %bitcast.13), custom_call_target="tpu_custom_call" | custom-call | tf_op jit(solution)/shard_map/pack/pallas_call | solution.py:80
  3.6 0.0 copy-start
  3.6 8.3 %all-to-all-start = ((bf16[8,528,256]{2,1,0:T(8,128)(2,1)}), bf16[8,528,256]{2,1,0:T(8,128)(2,1)S(1)}, u32[]{:S(2)}, u32[]{:S(2)}) async-start(bf16[8,528,256]{2,1,0:T(8,128)(2,1)} %pack.1), calls=%async_computation | async-start | bytes 4325376 | tf_op jit(solution)/shard_map/all_to_all | solution.py:225
  11.9 1.3 %dynamic_slice.6 = s32[1,1]{0,1:T(1,128)} dynamic-slice(s32[16,8]{0,1:T(8,128)} %param.15, s32[]{:T(128)S(6)} %select_n.10, s32[]{:T(128)S(6)} %select_n.11), dynamic_slice_sizes={1,1} | dynamic-slice | bytes 12 | tf_op jit(solution)/shard_map/dynamic_slice | solution.py:216
  13.9 0.0 copy-done
  13.9 0.1 reshape.13
  14.0 0.1 constant_dynamic-slice_fusion
  14.0 0.1 copy.13
  14.1 0.2 reduce_window_sum.14
  14.3 0.1 convert_reduce_fusion.docs_ref
  14.5 31.3 %all-to-all-done.in_ref = bf16[8,528,256]{2,1,0:T(8,128)(2,1)S(1)} async-done(((bf16[8,528,256]{2,1,0:T(8,128)(2,1)}), bf16[8,528,256]{2,1,0:T(8,128)(2,1)S(1)}, u32[]{:S(2)}, u32[]{:S(2)}) %all-to-all-start) | async-done | bytes 2162720 | tf_op jit(solution)/shard_map/all_to_all | solution.py:225
  45.8 3.2 %attend.1 = bf16[8,384,256]{2,1,0:T(8,128)(2,1)S(1)} custom-call(s32[1]{0:T(128)} %bitcast.1.swap_ref, s32[2,4]{1,0:T(2,128)S(1)} %convert_reduce_fusion.docs_ref, bf16[8,528,256]{2,1,0:T(8,128)(2,1)S(1)} %all-to-all-done.in_ref), custom_call_target="tpu_custom_call" | custom-call | flops 1342177280 | bytes 4194304 | tf_op jit(solution)/shard_map/attend/pallas_call | solution.py:167
  49.0 26.9 %all_to_all.10.in_ref = bf16[8,384,256]{2,1,0:T(8,128)(2,1)S(1)} all-to-all(bf16[8,384,256]{2,1,0:T(8,128)(2,1)S(1)} %attend.1), channel_id=1, replica_groups=mesh['side'=2,'low'=8,'bin'=8,'spot'=4] {'side','spot'}, dimensions={0} | all-to-all | bytes 3145728 | tf_op jit(solution)/shard_map/all_to_all | solution.py:226
  75.9 1.3 %unpack.1 = (bf16[1,128,2048]{2,1,0:T(8,128)(2,1)}, bf16[1,128,2048]{2,1,0:T(8,128)(2,1)}, bf16[1,128,2048]{2,1,0:T(8,128)(2,1)}) custom-call(bf16[8,384,256]{2,1,0:T(8,128)(2,1)S(1)} %all_to_all.10.in_ref), custom_call_target="tpu_custom_call" | custom-call | tf_op jit(solution)/shard_map/unpack/pallas_call | solution.py:201
Async XLA Ops:
  3.6 10.2 %copy-start = (s32[16,8,4]{0,2,1:T(4,128)S(1)}, s32[16,8,4]{0,2,1:T(4,128)}, u32[]{:S(2)}) copy-start(s32[16,8,4]{0,2,1:T(4,128)} %param.14) | copy-start | bytes 6148
  3.6 42.1 %all-to-all-start = ((bf16[8,528,256]{2,1,0:T(8,128)(2,1)}), bf16[8,528,256]{2,1,0:T(8,128)(2,1)S(1)}, u32[]{:S(2)}, u32[]{:S(2)}) async-start(bf16[8,528,256]{2,1,0:T(8,128)(2,1)} %pack.1), calls=%async_computation | async-start | bytes 4325376 | tf_op jit(solution)/shard_map/all_to_all | solution.py:225

commit v5 on v4

--- a/solution.py
+++ b/solution.py
@@ -13,6 +13,7 @@
 SIDES = 2
 SPOTS = 4
 TEAM = SIDES * SPOTS
+ORDER = (0, 2, 1, 3, 5, 7, 4, 6)
 STAT_ROWS = 16
 IN_ROWS = 4 * TOK + STAT_ROWS
 OUT_ROWS = 3 * TOK
@@ -101,17 +102,24 @@
     return jnp.dot(a, b, preferred_element_type=jnp.float32)
 
 
+def message_of(member):
+    return jnp.bitwise_xor(ORDER.index(member), (TEAM - 1) * (lax.axis_index("low") % 2))
+
+
 def attend_kernel(swap_ref, docs_ref, in_ref, out_ref):
     span = SPOTS * TOK
     per_member = in_ref.shape[2] // HEAD
-    swap = swap_ref[0]
+    swapped = swap_ref[0] != 0
+    places = [message_of(member) for member in range(TEAM)]
 
     def unit(side, lanes):
-        source = slice(side * SPOTS, (side + 1) * SPOTS)
-        target = jnp.bitwise_xor(side, swap) * SPOTS
+        own = places[side * SPOTS : (side + 1) * SPOTS]
+        other = places[(1 - side) * SPOTS : (2 - side) * SPOTS]
+        target = [jnp.where(swapped, theirs, ours) for ours, theirs in zip(own, other)]
 
         def whole(slot):
-            return in_ref[source, slot * TOK : (slot + 1) * TOK, lanes].reshape(span, HEAD)
+            rows = slice(slot * TOK, (slot + 1) * TOK)
+            return jnp.concatenate([in_ref[place, rows, lanes] for place in own], axis=0)
 
         q, k, v, g = (whole(slot) for slot in range(4))
         k_turned = k.T
@@ -121,7 +129,7 @@
             spots = range(first, first + QUERY_SPOTS)
             columns = slice(first * TOK, (first + QUERY_SPOTS) * TOK)
             stats = [
-                in_ref[side * SPOTS + spot, 4 * TOK :, lanes].astype(jnp.float32)
+                in_ref[own[spot], 4 * TOK :, lanes].astype(jnp.float32)
                 for spot in spots
             ]
             delta = jnp.concatenate([stat[1:2] for stat in stats], axis=1)
@@ -147,13 +155,13 @@
             dv = dv + nn(probs_low, g[columns])
             dq = (nn(k_turned, dscores) * ROOT).T.astype(jnp.bfloat16)
             for place, spot in enumerate(spots):
-                out_ref[target + spot, :TOK, lanes] = dq[place * TOK : (place + 1) * TOK]
+                out_ref[target[spot], :TOK, lanes] = dq[place * TOK : (place + 1) * TOK]
         dk = (dk * ROOT).astype(jnp.bfloat16)
         dv = dv.astype(jnp.bfloat16)
         for spot in range(SPOTS):
             rows = slice(spot * TOK, (spot + 1) * TOK)
-            out_ref[target + spot, TOK : 2 * TOK, lanes] = dk[rows]
-            out_ref[target + spot, 2 * TOK :, lanes] = dv[rows]
+            out_ref[target[spot], TOK : 2 * TOK, lanes] = dk[rows]
+            out_ref[target[spot], 2 * TOK :, lanes] = dv[rows]
 
     for side in range(SIDES):
         for head in range(per_member):
@@ -209,6 +217,20 @@
     )(in_vmem(messages))
 
 
+def exchange(messages):
+    axes = ("side", "low", "bin", "spot")
+    _, lows, bins, _ = (lax.axis_size(axis) for axis in axes)
+    teams = [
+        [
+            ((member // SPOTS * lows + low) * bins + place) * SPOTS + member % SPOTS
+            for member in (ORDER[::-1] if low % 2 else ORDER)
+        ]
+        for low in range(lows)
+        for place in range(bins)
+    ]
+    return lax.all_to_all(messages, axes, 0, 0, tiled=True, axis_index_groups=teams)
+
+
 def body(q, k, v, g, norm, delta, doc_lengths, bin_dest):
     groups = lax.axis_size("low")
     low = lax.axis_index("low")
@@ -220,11 +242,8 @@
         (ends[:, None, :] <= jnp.arange(SPOTS, dtype=jnp.int32)[None, :, None]).astype(jnp.int32),
         axis=2,
     )
-    team = ("side", "spot")
     packed = pack(q, k, v, g, jnp.transpose(norm[0]), jnp.transpose(delta[0]))
-    messages = lax.all_to_all(packed, team, 0, 0, tiled=True)
-    grads = lax.all_to_all(attend(swap, docs, messages), team, 0, 0, tiled=True)
-    return unpack(grads)
+    return unpack(exchange(attend(swap, docs, exchange(packed))))
 
 
 def solution(mesh):

time: 77.5 us -> 70.3 us (0.907)
  the two profiles are of different devices: /device:TPU:128 before, /device:TPU:504 now
where the time goes in v5:
time: 70.3 us; the launch traced here: 69.5 us
  blocking collectives  26.2 us (37%)
  waiting for transfers between devices  24.1 us (34%)
  starting transfers between devices  8.18 us (12%)
  Pallas kernels  7.85 us (11%)
  local copies, waits for them, and re-layouts  1.55 us (2%)
  between operations  1.32 us (2%)
    all_to_all x1, blocking collectives, exchange(): lax.all_to_all(messages, axes, 0, 0, tiled=True, axis_index_groups=teams)  26.2 us
    all_to_all x1, waiting for transfers between devices, exchange(): lax.all_to_all(messages, axes, 0, 0, tiled=True, axis_index_groups=teams)  24.1 us
    all_to_all x1, starting transfers between devices, exchange(): lax.all_to_all(messages, axes, 0, 0, tiled=True, axis_index_groups=teams)  8.18 us
    pallas_call x1, Pallas kernels, attend(): pl.pallas_call(attend_kernel, out_shape=pltpu.VMEM((TEAM, OUT_ROWS, messa...  3.54 us
    pallas_call x1, Pallas kernels, pack(): pl.pallas_call(pack_kernel, out_shape=pltpu.VMEM((TEAM, IN_ROWS, width),...  2.99 us
  transfers between devices with their start and end apart: 1, of which 1 were waited for; matrix products, arithmetic and copies ran while one was open for 3% of the time, Pallas kernels for 0%

profile of v5, /device:TPU:504, one launch (start us, length us, event | category | flops | bytes accessed | tf_op | source)
XLA Modules:
  0.0 69.5 jit_solution(16369306699656821529)
XLA Ops:
  0.6 3.0 %pack.1 = bf16[8,528,256]{2,1,0:T(8,128)(2,1)} custom-call(bf16[1,128,2048]{2,1,0:T(8,128)(2,1)} %q_ref.1, bf16[1,128,2048]{2,1,0:T(8,128)(2,1)} %k_ref.1, bf16[1,128,2048]{2,1,0:T(8,128)(2,1)} %v_ref.1, bf16[1,128,2048]{2,1,0:T(8,128)(2,1)} %g_ref.1, bf16[16,128]{1,0:T(8,128)(2,1)} %bitcast.12, bf16[16,128]{1,0:T(8,128)(2,1)} %bitcast.13), custom_call_target="tpu_custom_call" | custom-call | tf_op jit(solution)/shard_map/pack/pallas_call | solution.py:81
  3.6 0.0 copy-start
  3.6 8.2 %all-to-all-start = ((bf16[8,528,256]{2,1,0:T(8,128)(2,1)}), bf16[8,528,256]{2,1,0:T(8,128)(2,1)S(1)}, u32[]{:S(2)}, u32[]{:S(2)}) async-start(bf16[8,528,256]{2,1,0:T(8,128)(2,1)} %pack.1), calls=%async_computation | async-start | bytes 4325376 | tf_op jit(solution)/shard_map/all_to_all | solution.py:231
  11.8 1.3 %dynamic_slice.6 = s32[1,1]{0,1:T(1,128)} dynamic-slice(s32[16,8]{0,1:T(8,128)} %param.15, s32[]{:T(128)S(6)} %select_n.10, s32[]{:T(128)S(6)} %select_n.11), dynamic_slice_sizes={1,1} | dynamic-slice | bytes 12 | tf_op jit(solution)/shard_map/dynamic_slice | solution.py:238
  13.7 0.0 copy-done
  13.7 0.1 reshape.13
  13.8 0.1 constant_dynamic-slice_fusion
  13.9 0.1 copy.13
  14.0 0.2 reduce_window_sum.14
  14.2 0.1 convert_reduce_fusion.docs_ref
  14.4 24.1 %all-to-all-done.in_ref = bf16[8,528,256]{2,1,0:T(8,128)(2,1)S(1)} async-done(((bf16[8,528,256]{2,1,0:T(8,128)(2,1)}), bf16[8,528,256]{2,1,0:T(8,128)(2,1)S(1)}, u32[]{:S(2)}, u32[]{:S(2)}) %all-to-all-start) | async-done | bytes 2162720 | tf_op jit(solution)/shard_map/all_to_all | solution.py:231
  38.5 3.5 %attend.1 = bf16[8,384,256]{2,1,0:T(8,128)(2,1)S(1)} custom-call(s32[1]{0:T(128)} %bitcast.1.swap_ref, s32[2,4]{1,0:T(2,128)S(1)} %convert_reduce_fusion.docs_ref, bf16[8,528,256]{2,1,0:T(8,128)(2,1)S(1)} %all-to-all-done.in_ref), custom_call_target="tpu_custom_call" | custom-call | flops 1342177280 | bytes 4194304 | tf_op jit(solution)/shard_map/attend/pallas_call | solution.py:175
  42.0 26.2 %all_to_all.10.in_ref = bf16[8,384,256]{2,1,0:T(8,128)(2,1)S(1)} all-to-all(bf16[8,384,256]{2,1,0:T(8,128)(2,1)S(1)} %attend.1), channel_id=1, replica_groups={{0,2,1,3,257,259,256,258},{4,6,5,7,261,263,260,262},{8,10,9,11,265,267,..., dimensions={0} | all-to-all | bytes 3145728 | tf_op jit(solution)/shard_map/all_to_all | solution.py:231
  68.2 1.3 %unpack.1 = (bf16[1,128,2048]{2,1,0:T(8,128)(2,1)}, bf16[1,128,2048]{2,1,0:T(8,128)(2,1)}, bf16[1,128,2048]{2,1,0:T(8,128)(2,1)}) custom-call(bf16[8,384,256]{2,1,0:T(8,128)(2,1)S(1)} %all_to_all.10.in_ref), custom_call_target="tpu_custom_call" | custom-call | tf_op jit(solution)/shard_map/unpack/pallas_call | solution.py:209
Async XLA Ops:
  3.6 10.1 %copy-start = (s32[16,8,4]{0,2,1:T(4,128)S(1)}, s32[16,8,4]{0,2,1:T(4,128)}, u32[]{:S(2)}) copy-start(s32[16,8,4]{0,2,1:T(4,128)} %param.14) | copy-start | bytes 6148
  3.6 34.9 %all-to-all-start = ((bf16[8,528,256]{2,1,0:T(8,128)(2,1)}), bf16[8,528,256]{2,1,0:T(8,128)(2,1)S(1)}, u32[]{:S(2)}, u32[]{:S(2)}) async-start(bf16[8,528,256]{2,1,0:T(8,128)(2,1)} %pack.1), calls=%async_computation | async-start | bytes 4325376 | tf_op jit(solution)/shard_map/all_to_all | solution.py:231

commit v6 on v5

--- a/solution.py
+++ b/solution.py
@@ -13,9 +13,8 @@
 SIDES = 2
 SPOTS = 4
 TEAM = SIDES * SPOTS
-ORDER = (0, 2, 1, 3, 5, 7, 4, 6)
+ORDERS = ((0, 2, 1, 3, 5, 7, 4, 6), (0, 4, 2, 6, 3, 7, 1, 5))
 STAT_ROWS = 16
-IN_ROWS = 4 * TOK + STAT_ROWS
 OUT_ROWS = 3 * TOK
 MASKED = -1e30
 ROOT = 1.0 / math.sqrt(HEAD)
@@ -31,7 +30,7 @@
 
 
 def pack_kernel(q_ref, k_ref, v_ref, g_ref, norm_ref, delta_ref, out_ref, held, stats, sems, stat_sems):
-    width = out_ref.shape[2]
+    per_member = held.shape[2] // (TEAM * HEAD)
     stat_copies = start_all(
         [
             pltpu.make_async_copy(ref, stats.at[slot], stat_sems.at[slot])
@@ -49,17 +48,20 @@
     norm = stats[0].astype(jnp.float32)
     delta = stats[1].astype(jnp.float32)
     row = lax.broadcasted_iota(jnp.int32, (STAT_ROWS, HEAD), 0)
-    per_member = width // HEAD
-    for head in range(TEAM * per_member):
-        tile = jnp.where(row == 0, norm[head : head + 1], 0.0)
-        tile = jnp.where(row == 1, delta[head : head + 1], tile)
-        place = head % per_member * HEAD
-        out_ref[head // per_member, 4 * TOK :, place : place + HEAD] = tile.astype(jnp.bfloat16)
+    for member in range(TEAM):
+        tile = jnp.zeros((STAT_ROWS, HEAD), jnp.float32)
+        for place in range(per_member):
+            head = member * per_member + place
+            tile = jnp.where(row == 2 * place, norm[head : head + 1], tile)
+            tile = jnp.where(row == 2 * place + 1, delta[head : head + 1], tile)
+        out_ref[member, per_member * 4 * TOK :, :] = tile.astype(jnp.bfloat16)
     for slot, copy in enumerate(copies):
         copy.wait()
-        for member in range(TEAM):
-            out_ref[member, slot * TOK : (slot + 1) * TOK, :] = held[
-                slot, :, member * width : (member + 1) * width
+        for head in range(TEAM * per_member):
+            member, place = divmod(head, per_member)
+            first = (place * 4 + slot) * TOK
+            out_ref[member, first : first + TOK, :] = held[
+                slot, :, head * HEAD : (head + 1) * HEAD
             ]
 
 
@@ -77,10 +79,10 @@
 
 
 def pack(q, k, v, g, norm, delta):
-    width = q.shape[2] // TEAM
+    rows = q.shape[2] // (TEAM * HEAD) * 4 * TOK + STAT_ROWS
     return pl.pallas_call(
         pack_kernel,
-        out_shape=pltpu.VMEM((TEAM, IN_ROWS, width), jnp.bfloat16),
+        out_shape=pltpu.VMEM((TEAM, rows, HEAD), jnp.bfloat16),
         in_specs=[ANYWHERE] * 6,
         out_specs=LOCAL,
         scratch_shapes=[
@@ -103,23 +105,27 @@
 
 
 def message_of(member):
-    return jnp.bitwise_xor(ORDER.index(member), (TEAM - 1) * (lax.axis_index("low") % 2))
+    low = lax.axis_index("low")
+    first, second = (order.index(member) for order in ORDERS)
+    place = jnp.where(low // 2 % 2 == 0, first, second)
+    return jnp.bitwise_xor(place, (TEAM - 1) * (low % 2))
 
 
 def attend_kernel(swap_ref, docs_ref, in_ref, out_ref):
     span = SPOTS * TOK
-    per_member = in_ref.shape[2] // HEAD
+    per_member = out_ref.shape[2] // HEAD
     swapped = swap_ref[0] != 0
     places = [message_of(member) for member in range(TEAM)]
 
-    def unit(side, lanes):
+    def unit(side, head):
+        lanes = slice(head * HEAD, (head + 1) * HEAD)
         own = places[side * SPOTS : (side + 1) * SPOTS]
         other = places[(1 - side) * SPOTS : (2 - side) * SPOTS]
         target = [jnp.where(swapped, theirs, ours) for ours, theirs in zip(own, other)]
 
         def whole(slot):
-            rows = slice(slot * TOK, (slot + 1) * TOK)
-            return jnp.concatenate([in_ref[place, rows, lanes] for place in own], axis=0)
+            rows = slice((head * 4 + slot) * TOK, (head * 4 + slot + 1) * TOK)
+            return jnp.concatenate([in_ref[place, rows, :] for place in own], axis=0)
 
         q, k, v, g = (whole(slot) for slot in range(4))
         k_turned = k.T
@@ -129,10 +135,11 @@
             spots = range(first, first + QUERY_SPOTS)
             columns = slice(first * TOK, (first + QUERY_SPOTS) * TOK)
             stats = [
-                in_ref[own[spot], 4 * TOK :, lanes].astype(jnp.float32)
+                in_ref[own[spot], per_member * 4 * TOK :, :].astype(jnp.float32)
                 for spot in spots
             ]
-            delta = jnp.concatenate([stat[1:2] for stat in stats], axis=1)
+            norms = [stat[2 * head : 2 * head + 1] for stat in stats]
+            delta = jnp.concatenate([stat[2 * head + 1 : 2 * head + 2] for stat in stats], axis=1)
             scores = nt(k, q[columns])
             dprobs = nt(v, g[columns])
             probs_low, dscores = [], []
@@ -141,8 +148,8 @@
                 key_doc = docs_ref[side, key_spot]
                 bias = jnp.concatenate(
                     [
-                        jnp.where(docs_ref[side, spot] == key_doc, stat[0:1] * -LOG2E, MASKED)
-                        for spot, stat in zip(spots, stats)
+                        jnp.where(docs_ref[side, spot] == key_doc, norm * -LOG2E, MASKED)
+                        for spot, norm in zip(spots, norms)
                     ],
                     axis=1,
                 )
@@ -165,16 +172,17 @@
 
     for side in range(SIDES):
         for head in range(per_member):
-            unit(side, slice(head * HEAD, (head + 1) * HEAD))
+            unit(side, head)
 
 
 def attend(swap, docs, messages):
     span = SPOTS * TOK
-    units = SIDES * messages.shape[2] // HEAD
+    per_member = messages.shape[1] // (4 * TOK)
+    units = SIDES * per_member
     scalars = pl.BlockSpec(memory_space=pltpu.SMEM)
     return pl.pallas_call(
         attend_kernel,
-        out_shape=pltpu.VMEM((TEAM, OUT_ROWS, messages.shape[2]), jnp.bfloat16),
+        out_shape=pltpu.VMEM((TEAM, OUT_ROWS, per_member * HEAD), jnp.bfloat16),
         in_specs=[scalars, scalars, LOCAL],
         out_specs=LOCAL,
         compiler_params=PARAMS,
@@ -223,7 +231,7 @@
     teams = [
         [
             ((member // SPOTS * lows + low) * bins + place) * SPOTS + member % SPOTS
-            for member in (ORDER[::-1] if low % 2 else ORDER)
+            for member in ORDERS[low // 2 % 2][:: -1 if low % 2 else 1]
         ]
         for low in range(lows)
         for place in range(bins)

time: 70.3 us -> 69.6 us (0.990)
  no operation moved by 1% of the time
where the time goes in v6:
time: 69.6 us; the launch traced here: 69.3 us
  blocking collectives  26.2 us (38%)
  waiting for transfers between devices  23.8 us (34%)
  starting transfers between devices  8.18 us (12%)
  Pallas kernels  7.91 us (11%)
  local copies, waits for them, and re-layouts  1.55 us (2%)
  between operations  1.32 us (2%)
    all_to_all x1, blocking collectives, exchange(): lax.all_to_all(messages, axes, 0, 0, tiled=True, axis_index_groups=teams)  26.2 us
    all_to_all x1, waiting for transfers between devices, exchange(): lax.all_to_all(messages, axes, 0, 0, tiled=True, axis_index_groups=teams)  23.8 us
    all_to_all x1, starting transfers between devices, exchange(): lax.all_to_all(messages, axes, 0, 0, tiled=True, axis_index_groups=teams)  8.18 us
    pallas_call x1, Pallas kernels, attend(): pl.pallas_call(attend_kernel, out_shape=pltpu.VMEM((TEAM, OUT_ROWS, per_m...  3.54 us
    pallas_call x1, Pallas kernels, pack(): pl.pallas_call(pack_kernel, out_shape=pltpu.VMEM((TEAM, rows, HEAD), jnp....  3.04 us
  transfers between devices with their start and end apart: 1, of which 1 were waited for; matrix products, arithmetic and copies ran while one was open for 3% of the time, Pallas kernels for 0%

profile of v6, /device:TPU:504, one launch (start us, length us, event | category | flops | bytes accessed | tf_op | source)
XLA Modules:
  0.0 69.3 jit_solution(8118486511344226133)
XLA Ops:
  0.6 3.0 %pack.1 = bf16[8,1040,128]{2,1,0:T(8,128)(2,1)} custom-call(bf16[1,128,2048]{2,1,0:T(8,128)(2,1)} %q_ref.1, bf16[1,128,2048]{2,1,0:T(8,128)(2,1)} %k_ref.1, bf16[1,128,2048]{2,1,0:T(8,128)(2,1)} %v_ref.1, bf16[1,128,2048]{2,1,0:T(8,128)(2,1)} %g_ref.1, bf16[16,128]{1,0:T(8,128)(2,1)} %bitcast.12, bf16[16,128]{1,0:T(8,128)(2,1)} %bitcast.13), custom_call_target="tpu_custom_call" | custom-call | tf_op jit(solution)/shard_map/pack/pallas_call | solution.py:83
  3.7 0.0 copy-start
  3.7 8.2 %all-to-all-start = ((bf16[8,1040,128]{2,1,0:T(8,128)(2,1)}), bf16[8,1040,128]{2,1,0:T(8,128)(2,1)S(1)}, u32[]{:S(2)}, u32[]{:S(2)}) async-start(bf16[8,1040,128]{2,1,0:T(8,128)(2,1)} %pack.1), calls=%async_computation | async-start | bytes 4259840 | tf_op jit(solution)/shard_map/all_to_all | solution.py:239
  11.9 1.3 %dynamic_slice.6 = s32[1,1]{0,1:T(1,128)} dynamic-slice(s32[16,8]{0,1:T(8,128)} %param.15, s32[]{:T(128)S(6)} %select_n.10, s32[]{:T(128)S(6)} %select_n.11), dynamic_slice_sizes={1,1} | dynamic-slice | bytes 12 | tf_op jit(solution)/shard_map/dynamic_slice | solution.py:246
  13.8 0.0 copy-done
  13.8 0.1 reshape.13
  13.9 0.1 constant_dynamic-slice_fusion
  14.0 0.1 copy.13
  14.1 0.2 reduce_window_sum.14
  14.3 0.1 convert_reduce_fusion.docs_ref
  14.4 23.8 %all-to-all-done.in_ref = bf16[8,1040,128]{2,1,0:T(8,128)(2,1)S(1)} async-done(((bf16[8,1040,128]{2,1,0:T(8,128)(2,1)}), bf16[8,1040,128]{2,1,0:T(8,128)(2,1)S(1)}, u32[]{:S(2)}, u32[]{:S(2)}) %all-to-all-start) | async-done | bytes 2129952 | tf_op jit(solution)/shard_map/all_to_all | solution.py:239
  38.2 3.5 %attend.1 = bf16[8,384,256]{2,1,0:T(8,128)(2,1)S(1)} custom-call(s32[1]{0:T(128)} %bitcast.1.swap_ref, s32[2,4]{1,0:T(2,128)S(1)} %convert_reduce_fusion.docs_ref, bf16[8,1040,128]{2,1,0:T(8,128)(2,1)S(1)} %all-to-all-done.in_ref), custom_call_target="tpu_custom_call" | custom-call | flops 1342177280 | bytes 4194304 | tf_op jit(solution)/shard_map/attend/pallas_call | solution.py:183
  41.8 26.2 %all_to_all.10.in_ref = bf16[8,384,256]{2,1,0:T(8,128)(2,1)S(1)} all-to-all(bf16[8,384,256]{2,1,0:T(8,128)(2,1)S(1)} %attend.1), channel_id=1, replica_groups={{0,2,1,3,257,259,256,258},{4,6,5,7,261,263,260,262},{8,10,9,11,265,267,..., dimensions={0} | all-to-all | bytes 3145728 | tf_op jit(solution)/shard_map/all_to_all | solution.py:239
  67.9 1.3 %unpack.1 = (bf16[1,128,2048]{2,1,0:T(8,128)(2,1)}, bf16[1,128,2048]{2,1,0:T(8,128)(2,1)}, bf16[1,128,2048]{2,1,0:T(8,128)(2,1)}) custom-call(bf16[8,384,256]{2,1,0:T(8,128)(2,1)S(1)} %all_to_all.10.in_ref), custom_call_target="tpu_custom_call" | custom-call | tf_op jit(solution)/shard_map/unpack/pallas_call | solution.py:217
Async XLA Ops:
  3.7 10.1 %copy-start = (s32[16,8,4]{0,2,1:T(4,128)S(1)}, s32[16,8,4]{0,2,1:T(4,128)}, u32[]{:S(2)}) copy-start(s32[16,8,4]{0,2,1:T(4,128)} %param.14) | copy-start | bytes 6148
  3.7 34.5 %all-to-all-start = ((bf16[8,1040,128]{2,1,0:T(8,128)(2,1)}), bf16[8,1040,128]{2,1,0:T(8,128)(2,1)S(1)}, u32[]{:S(2)}, u32[]{:S(2)}) async-start(bf16[8,1040,128]{2,1,0:T(8,128)(2,1)} %pack.1), calls=%async_computation | async-start | bytes 4259840 | tf_op jit(solution)/shard_map/all_to_all | solution.py:239

commit v7 on v6

--- a/solution.py
+++ b/solution.py
@@ -19,7 +19,6 @@
 MASKED = -1e30
 ROOT = 1.0 / math.sqrt(HEAD)
 LOG2E = math.log2(math.e)
-QUERY_SPOTS = 4
 VMEM_LIMIT = 24 << 20
 
 
@@ -117,62 +116,57 @@
     swapped = swap_ref[0] != 0
     places = [message_of(member) for member in range(TEAM)]
 
-    def unit(side, head):
+    def whole(side, head, slot):
+        rows = slice((head * 4 + slot) * TOK, (head * 4 + slot + 1) * TOK)
+        own = places[side * SPOTS : (side + 1) * SPOTS]
+        return jnp.concatenate([in_ref[place, rows, :] for place in own], axis=0)
+
+    def multiply(side, head):
+        q, k, v, g = (whole(side, head, slot) for slot in range(4))
+        return nt(k, q), nt(v, g)
+
+    def weigh(side, head, scores, dprobs):
+        own = places[side * SPOTS : (side + 1) * SPOTS]
+        stats = [in_ref[place, per_member * 4 * TOK :, :].astype(jnp.float32) for place in own]
+        norms = [stat[2 * head : 2 * head + 1] * -LOG2E for stat in stats]
+        delta = jnp.concatenate([stat[2 * head + 1 : 2 * head + 2] for stat in stats], axis=1)
+        probs_low, dscores = [], []
+        for key_spot in range(SPOTS):
+            rows = slice(key_spot * TOK, (key_spot + 1) * TOK)
+            key_doc = docs_ref[side, key_spot]
+            bias = jnp.concatenate(
+                [
+                    jnp.where(docs_ref[side, spot] == key_doc, norm, MASKED)
+                    for spot, norm in enumerate(norms)
+                ],
+                axis=1,
+            )
+            probs = jnp.exp2(scores[rows] * (ROOT * LOG2E) + bias)
+            probs_low.append(probs.astype(jnp.bfloat16))
+            dscores.append((probs * (dprobs[rows] - delta)).astype(jnp.bfloat16))
+        return jnp.concatenate(probs_low, axis=0), jnp.concatenate(dscores, axis=0)
+
+    def finish(side, head, probs_low, dscores):
         lanes = slice(head * HEAD, (head + 1) * HEAD)
         own = places[side * SPOTS : (side + 1) * SPOTS]
         other = places[(1 - side) * SPOTS : (2 - side) * SPOTS]
-        target = [jnp.where(swapped, theirs, ours) for ours, theirs in zip(own, other)]
-
-        def whole(slot):
-            rows = slice((head * 4 + slot) * TOK, (head * 4 + slot + 1) * TOK)
-            return jnp.concatenate([in_ref[place, rows, :] for place in own], axis=0)
-
-        q, k, v, g = (whole(slot) for slot in range(4))
-        k_turned = k.T
-        dk = jnp.zeros((span, HEAD), jnp.float32)
-        dv = jnp.zeros((span, HEAD), jnp.float32)
-        for first in range(0, SPOTS, QUERY_SPOTS):
-            spots = range(first, first + QUERY_SPOTS)
-            columns = slice(first * TOK, (first + QUERY_SPOTS) * TOK)
-            stats = [
-                in_ref[own[spot], per_member * 4 * TOK :, :].astype(jnp.float32)
-                for spot in spots
-            ]
-            norms = [stat[2 * head : 2 * head + 1] for stat in stats]
-            delta = jnp.concatenate([stat[2 * head + 1 : 2 * head + 2] for stat in stats], axis=1)
-            scores = nt(k, q[columns])
-            dprobs = nt(v, g[columns])
-            probs_low, dscores = [], []
-            for key_spot in range(SPOTS):
-                rows = slice(key_spot * TOK, (key_spot + 1) * TOK)
-                key_doc = docs_ref[side, key_spot]
-                bias = jnp.concatenate(
-                    [
-                        jnp.where(docs_ref[side, spot] == key_doc, norm * -LOG2E, MASKED)
-                        for spot, norm in zip(spots, norms)
-                    ],
-                    axis=1,
-                )
-                probs = jnp.exp2(scores[rows] * (ROOT * LOG2E) + bias)
-                probs_low.append(probs.astype(jnp.bfloat16))
-                dscores.append((probs * (dprobs[rows] - delta)).astype(jnp.bfloat16))
-            probs_low = jnp.concatenate(probs_low, axis=0)
-            dscores = jnp.concatenate(dscores, axis=0)
-            dk = dk + nn(dscores, q[columns])
-            dv = dv + nn(probs_low, g[columns])
-            dq = (nn(k_turned, dscores) * ROOT).T.astype(jnp.bfloat16)
-            for place, spot in enumerate(spots):
-                out_ref[target[spot], :TOK, lanes] = dq[place * TOK : (place + 1) * TOK]
-        dk = (dk * ROOT).astype(jnp.bfloat16)
-        dv = dv.astype(jnp.bfloat16)
+        q, k, _, g = (whole(side, head, slot) for slot in range(4))
+        dq = (nn(k.T, dscores) * ROOT).T.astype(jnp.bfloat16)
+        dk = (nn(dscores, q) * ROOT).astype(jnp.bfloat16)
+        dv = nn(probs_low, g).astype(jnp.bfloat16)
         for spot in range(SPOTS):
+            target = jnp.where(swapped, other[spot], own[spot])
             rows = slice(spot * TOK, (spot + 1) * TOK)
-            out_ref[target[spot], TOK : 2 * TOK, lanes] = dk[rows]
-            out_ref[target[spot], 2 * TOK :, lanes] = dv[rows]
-
-    for side in range(SIDES):
-        for head in range(per_member):
-            unit(side, head)
+            for slot, grad in enumerate((dq, dk, dv)):
+                out_ref[target, slot * TOK : (slot + 1) * TOK, lanes] = grad[rows]
+
+    units = [(side, head) for side in range(SIDES) for head in range(per_member)]
+    ahead = multiply(*units[0])
+    for number, unit in enumerate(units):
+        products = ahead
+        if number + 1 < len(units):
+            ahead = multiply(*units[number + 1])
+        finish(*unit, *weigh(*unit, *products))
 
 
 def attend(swap, docs, messages):

time: 69.6 us -> 69.3 us (level)
  no operation moved by 1% of the time
where the time goes in v7:
time: 69.3 us; the launch traced here: 69 us
  blocking collectives  26.2 us (38%)
  waiting for transfers between devices  23.8 us (34%)
  starting transfers between devices  8.18 us (12%)
  Pallas kernels  7.68 us (11%)
  local copies, waits for them, and re-layouts  1.55 us (2%)
  between operations  1.32 us (2%)
    all_to_all x1, blocking collectives, exchange(): lax.all_to_all(messages, axes, 0, 0, tiled=True, axis_index_groups=teams)  26.2 us
    all_to_all x1, waiting for transfers between devices, exchange(): lax.all_to_all(messages, axes, 0, 0, tiled=True, axis_index_groups=teams)  23.8 us
    all_to_all x1, starting transfers between devices, exchange(): lax.all_to_all(messages, axes, 0, 0, tiled=True, axis_index_groups=teams)  8.18 us
    pallas_call x1, Pallas kernels, attend(): pl.pallas_call(attend_kernel, out_shape=pltpu.VMEM((TEAM, OUT_ROWS, per_m...  3.32 us
    pallas_call x1, Pallas kernels, pack(): pl.pallas_call(pack_kernel, out_shape=pltpu.VMEM((TEAM, rows, HEAD), jnp....  3.04 us
  transfers between devices with their start and end apart: 1, of which 1 were waited for; matrix products, arithmetic and copies ran while one was open for 3% of the time, Pallas kernels for 0%

profile of v7, /device:TPU:504, one launch (start us, length us, event | category | flops | bytes accessed | tf_op | source)
XLA Modules:
  0.0 69.0 jit_solution(9652176426372598668)
XLA Ops:
  0.6 3.0 %pack.1 = bf16[8,1040,128]{2,1,0:T(8,128)(2,1)} custom-call(bf16[1,128,2048]{2,1,0:T(8,128)(2,1)} %q_ref.1, bf16[1,128,2048]{2,1,0:T(8,128)(2,1)} %k_ref.1, bf16[1,128,2048]{2,1,0:T(8,128)(2,1)} %v_ref.1, bf16[1,128,2048]{2,1,0:T(8,128)(2,1)} %g_ref.1, bf16[16,128]{1,0:T(8,128)(2,1)} %bitcast.12, bf16[16,128]{1,0:T(8,128)(2,1)} %bitcast.13), custom_call_target="tpu_custom_call" | custom-call | tf_op jit(solution)/shard_map/pack/pallas_call | solution.py:82
  3.7 0.0 copy-start
  3.7 8.2 %all-to-all-start = ((bf16[8,1040,128]{2,1,0:T(8,128)(2,1)}), bf16[8,1040,128]{2,1,0:T(8,128)(2,1)S(1)}, u32[]{:S(2)}, u32[]{:S(2)}) async-start(bf16[8,1040,128]{2,1,0:T(8,128)(2,1)} %pack.1), calls=%async_computation | async-start | bytes 4259840 | tf_op jit(solution)/shard_map/all_to_all | solution.py:233
  11.9 1.3 %dynamic_slice.6 = s32[1,1]{0,1:T(1,128)} dynamic-slice(s32[16,8]{0,1:T(8,128)} %param.15, s32[]{:T(128)S(6)} %select_n.10, s32[]{:T(128)S(6)} %select_n.11), dynamic_slice_sizes={1,1} | dynamic-slice | bytes 12 | tf_op jit(solution)/shard_map/dynamic_slice | solution.py:240
  13.8 0.0 copy-done
  13.8 0.1 reshape.13
  13.9 0.1 constant_dynamic-slice_fusion
  14.0 0.1 copy.13
  14.1 0.2 reduce_window_sum.14
  14.3 0.1 convert_reduce_fusion.docs_ref
  14.4 23.8 %all-to-all-done.in_ref = bf16[8,1040,128]{2,1,0:T(8,128)(2,1)S(1)} async-done(((bf16[8,1040,128]{2,1,0:T(8,128)(2,1)}), bf16[8,1040,128]{2,1,0:T(8,128)(2,1)S(1)}, u32[]{:S(2)}, u32[]{:S(2)}) %all-to-all-start) | async-done | bytes 2129952 | tf_op jit(solution)/shard_map/all_to_all | solution.py:233
  38.2 3.3 %attend.1 = bf16[8,384,256]{2,1,0:T(8,128)(2,1)S(1)} custom-call(s32[1]{0:T(128)} %bitcast.1.swap_ref, s32[2,4]{1,0:T(2,128)S(1)} %convert_reduce_fusion.docs_ref, bf16[8,1040,128]{2,1,0:T(8,128)(2,1)S(1)} %all-to-all-done.in_ref), custom_call_target="tpu_custom_call" | custom-call | flops 1342177280 | bytes 4194304 | tf_op jit(solution)/shard_map/attend/pallas_call | solution.py:177
  41.5 26.2 %all_to_all.10.in_ref = bf16[8,384,256]{2,1,0:T(8,128)(2,1)S(1)} all-to-all(bf16[8,384,256]{2,1,0:T(8,128)(2,1)S(1)} %attend.1), channel_id=1, replica_groups={{0,2,1,3,257,259,256,258},{4,6,5,7,261,263,260,262},{8,10,9,11,265,267,..., dimensions={0} | all-to-all | bytes 3145728 | tf_op jit(solution)/shard_map/all_to_all | solution.py:233
  67.7 1.3 %unpack.1 = (bf16[1,128,2048]{2,1,0:T(8,128)(2,1)}, bf16[1,128,2048]{2,1,0:T(8,128)(2,1)}, bf16[1,128,2048]{2,1,0:T(8,128)(2,1)}) custom-call(bf16[8,384,256]{2,1,0:T(8,128)(2,1)S(1)} %all_to_all.10.in_ref), custom_call_target="tpu_custom_call" | custom-call | tf_op jit(solution)/shard_map/unpack/pallas_call | solution.py:211
Async XLA Ops:
  3.7 10.1 %copy-start = (s32[16,8,4]{0,2,1:T(4,128)S(1)}, s32[16,8,4]{0,2,1:T(4,128)}, u32[]{:S(2)}) copy-start(s32[16,8,4]{0,2,1:T(4,128)} %param.14) | copy-start | bytes 6148
  3.7 34.5 %all-to-all-start = ((bf16[8,1040,128]{2,1,0:T(8,128)(2,1)}), bf16[8,1040,128]{2,1,0:T(8,128)(2,1)S(1)}, u32[]{:S(2)}, u32[]{:S(2)}) async-start(bf16[8,1040,128]{2,1,0:T(8,128)(2,1)} %pack.1), calls=%async_computation | async-start | bytes 4259840 | tf_op jit(solution)/shard_map/all_to_all | solution.py:233

commit v8 on v7

--- a/solution.py
+++ b/solution.py
@@ -161,12 +161,15 @@
                 out_ref[target, slot * TOK : (slot + 1) * TOK, lanes] = grad[rows]
 
     units = [(side, head) for side in range(SIDES) for head in range(per_member)]
-    ahead = multiply(*units[0])
+    ahead, weights = multiply(*units[0]), None
     for number, unit in enumerate(units):
         products = ahead
         if number + 1 < len(units):
             ahead = multiply(*units[number + 1])
-        finish(*unit, *weigh(*unit, *products))
+        if weights is not None:
+            finish(*units[number - 1], *weights)
+        weights = weigh(*unit, *products)
+    finish(*units[-1], *weights)
 
 
 def attend(swap, docs, messages):

time: 69.3 us -> 69.3 us (level)
  no operation moved by 1% of the time
where the time goes in v8:
time: 69.3 us; the launch traced here: 69 us
  blocking collectives  26.2 us (38%)
  waiting for transfers between devices  23.8 us (34%)
  starting transfers between devices  8.18 us (12%)
  Pallas kernels  7.67 us (11%)
  local copies, waits for them, and re-layouts  1.55 us (2%)
  between operations  1.32 us (2%)
    all_to_all x1, blocking collectives, exchange(): lax.all_to_all(messages, axes, 0, 0, tiled=True, axis_index_groups=teams)  26.2 us
    all_to_all x1, waiting for transfers between devices, exchange(): lax.all_to_all(messages, axes, 0, 0, tiled=True, axis_index_groups=teams)  23.8 us
    all_to_all x1, starting transfers between devices, exchange(): lax.all_to_all(messages, axes, 0, 0, tiled=True, axis_index_groups=teams)  8.18 us
    pallas_call x1, Pallas kernels, attend(): pl.pallas_call(attend_kernel, out_shape=pltpu.VMEM((TEAM, OUT_ROWS, per_m...  3.3 us
    pallas_call x1, Pallas kernels, pack(): pl.pallas_call(pack_kernel, out_shape=pltpu.VMEM((TEAM, rows, HEAD), jnp....  3.04 us
  transfers between devices with their start and end apart: 1, of which 1 were waited for; matrix products, arithmetic and copies ran while one was open for 3% of the time, Pallas kernels for 0%

profile of v8, /device:TPU:504, one launch (start us, length us, event | category | flops | bytes accessed | tf_op | source)
XLA Modules:
  0.0 69.0 jit_solution(7878519260418012498)
XLA Ops:
  0.6 3.0 %pack.1 = bf16[8,1040,128]{2,1,0:T(8,128)(2,1)} custom-call(bf16[1,128,2048]{2,1,0:T(8,128)(2,1)} %q_ref.1, bf16[1,128,2048]{2,1,0:T(8,128)(2,1)} %k_ref.1, bf16[1,128,2048]{2,1,0:T(8,128)(2,1)} %v_ref.1, bf16[1,128,2048]{2,1,0:T(8,128)(2,1)} %g_ref.1, bf16[16,128]{1,0:T(8,128)(2,1)} %bitcast.12, bf16[16,128]{1,0:T(8,128)(2,1)} %bitcast.13), custom_call_target="tpu_custom_call" | custom-call | tf_op jit(solution)/shard_map/pack/pallas_call | solution.py:82
  3.7 0.0 copy-start
  3.7 8.2 %all-to-all-start = ((bf16[8,1040,128]{2,1,0:T(8,128)(2,1)}), bf16[8,1040,128]{2,1,0:T(8,128)(2,1)S(1)}, u32[]{:S(2)}, u32[]{:S(2)}) async-start(bf16[8,1040,128]{2,1,0:T(8,128)(2,1)} %pack.1), calls=%async_computation | async-start | bytes 4259840 | tf_op jit(solution)/shard_map/all_to_all | solution.py:236
  11.9 1.3 %dynamic_slice.6 = s32[1,1]{0,1:T(1,128)} dynamic-slice(s32[16,8]{0,1:T(8,128)} %param.15, s32[]{:T(128)S(6)} %select_n.10, s32[]{:T(128)S(6)} %select_n.11), dynamic_slice_sizes={1,1} | dynamic-slice | bytes 12 | tf_op jit(solution)/shard_map/dynamic_slice | solution.py:243
  13.8 0.0 copy-done
  13.8 0.1 reshape.13
  13.9 0.1 constant_dynamic-slice_fusion
  14.0 0.1 copy.13
  14.1 0.2 reduce_window_sum.14
  14.3 0.1 convert_reduce_fusion.docs_ref
  14.4 23.8 %all-to-all-done.in_ref = bf16[8,1040,128]{2,1,0:T(8,128)(2,1)S(1)} async-done(((bf16[8,1040,128]{2,1,0:T(8,128)(2,1)}), bf16[8,1040,128]{2,1,0:T(8,128)(2,1)S(1)}, u32[]{:S(2)}, u32[]{:S(2)}) %all-to-all-start) | async-done | bytes 2129952 | tf_op jit(solution)/shard_map/all_to_all | solution.py:236
  38.2 3.3 %attend.1 = bf16[8,384,256]{2,1,0:T(8,128)(2,1)S(1)} custom-call(s32[1]{0:T(128)} %bitcast.1.swap_ref, s32[2,4]{1,0:T(2,128)S(1)} %convert_reduce_fusion.docs_ref, bf16[8,1040,128]{2,1,0:T(8,128)(2,1)S(1)} %all-to-all-done.in_ref), custom_call_target="tpu_custom_call" | custom-call | flops 1342177280 | bytes 4194304 | tf_op jit(solution)/shard_map/attend/pallas_call | solution.py:180
  41.5 26.2 %all_to_all.10.in_ref = bf16[8,384,256]{2,1,0:T(8,128)(2,1)S(1)} all-to-all(bf16[8,384,256]{2,1,0:T(8,128)(2,1)S(1)} %attend.1), channel_id=1, replica_groups={{0,2,1,3,257,259,256,258},{4,6,5,7,261,263,260,262},{8,10,9,11,265,267,..., dimensions={0} | all-to-all | bytes 3145728 | tf_op jit(solution)/shard_map/all_to_all | solution.py:236
  67.7 1.3 %unpack.1 = (bf16[1,128,2048]{2,1,0:T(8,128)(2,1)}, bf16[1,128,2048]{2,1,0:T(8,128)(2,1)}, bf16[1,128,2048]{2,1,0:T(8,128)(2,1)}) custom-call(bf16[8,384,256]{2,1,0:T(8,128)(2,1)S(1)} %all_to_all.10.in_ref), custom_call_target="tpu_custom_call" | custom-call | tf_op jit(solution)/shard_map/unpack/pallas_call | solution.py:214
Async XLA Ops:
  3.7 10.1 %copy-start = (s32[16,8,4]{0,2,1:T(4,128)S(1)}, s32[16,8,4]{0,2,1:T(4,128)}, u32[]{:S(2)}) copy-start(s32[16,8,4]{0,2,1:T(4,128)} %param.14) | copy-start | bytes 6148
  3.7 34.5 %all-to-all-start = ((bf16[8,1040,128]{2,1,0:T(8,128)(2,1)}), bf16[8,1040,128]{2,1,0:T(8,128)(2,1)S(1)}, u32[]{:S(2)}, u32[]{:S(2)}) async-start(bf16[8,1040,128]{2,1,0:T(8,128)(2,1)} %pack.1), calls=%async_computation | async-start | bytes 4259840 | tf_op jit(solution)/shard_map/all_to_all | solution.py:236
